TPU v7x, 32 devices: a whole 2x2x4 slice. The times are simulated.
32 devices in a mesh: dp: 8 (over z, y), tensor: 4 (over x, core).
Axes of the slice: x: 2, y: 2, z: 4, core: 2. Of those that a mesh axis runs over, the one named last changes fastest.
Arguments:
- queries: bfloat16 [4096, 3072], P('dp', 'tensor'), may hold values from -6 to 6
- keys: bfloat16 [4096, 3072], P('dp', 'tensor'), may hold values from -6 to 6
- values: bfloat16 [4096, 3072], P('dp', 'tensor'), may hold values from -6 to 6
- out_grad: bfloat16 [4096, 3072], P('dp', 'tensor'), may hold values from -6 to 6
- lengths: int32 [32], replicated, may hold values from 1 to 512, 4096 in all
Outputs:
- attn_out: bfloat16 [4096, 3072], P('dp', 'tensor')
- query_grad: bfloat16 [4096, 3072], P('dp', 'tensor')
- key_grad: bfloat16 [4096, 3072], P('dp', 'tensor')
- value_grad: bfloat16 [4096, 3072], P('dp', 'tensor')
Inputs may be any that keep to these rules, and one draw needn't show every extreme that they name: `lengths`: 32 token counts that sum to 4096, at least one image 512 long.
All inputs are finite; a program needn't handle non-finite values.
Results may differ from a plain program's by a relative error of at most 0.012.
Values may be sent and summed in bfloat16 or wider, within the bound.
No kernel may reach another device: no remote copies, remote signals or barrier semaphores. Data moves between devices by JAX's collectives and lax.ppermute only.
A program may use at most 64 MiB of HBM per device.

v0:
```python
import functools
import math

import jax
import jax.numpy as jnp
from jax import lax
from jax.experimental import pallas as pl
from jax.experimental.pallas import tpu as pltpu
from jax.sharding import PartitionSpec as P

HEAD_DIM = 128
TILE = 16
BLOCK = 64
LOCAL_CHUNK = 256
CROSSING_CHUNK = 512
FACTOR = 1.0 / math.sqrt(HEAD_DIM)
LOG2E = 1.4426950408889634
VMEM_LIMIT = 32 * 1024 * 1024
PACK_VMEM_LIMIT = 60 * 1024 * 1024

(A_BELOW, C_BELOW, HERE_BELOW, THERE_BELOW, A_ABOVE, C_ABOVE, HERE_ABOVE, THERE_ABOVE,
 DOWN_LEVEL, UP_LEVEL) = range(10)

LEVEL_UNITS = ()


def round_up(value):
    return (value + (TILE - 1)) // TILE * TILE


def worst_case_rows(rows, heads):
    worst = 0
    for before in range(TILE, rows + 1, TILE):
        for after in range(TILE, rows + TILE - before + 1, TILE):
            needed = min(max(after * low, before * (heads - low)) for low in range(heads + 1))
            worst = max(worst, needed)
    return worst


def size_levels(rows, heads):
    unit = rows * heads // 48
    most = worst_case_rows(rows, heads)
    return tuple(sorted(level * unit for level in LEVEL_UNITS if level * unit < most)) + (most,)


def size_menu(levels):
    count = len(levels)
    pairs = [(down, up) for down in range(count) for up in range(count)]
    return sorted(pairs, key=lambda pair: (levels[pair[0]] + levels[pair[1]], pair))


def make_plan(heads, rows, blocks, levels, lengths, plan, down_choice, up_choice, before_edge, after_edge):
    menu = size_menu(levels)

    def clear(edge, carry):
        before_edge[edge] = 0
        after_edge[edge] = 0
        return carry

    lax.fori_loop(0, blocks + 1, clear, 0)

    def place(image, start):
        end = start + lengths[image]
        edge = (end - 1) // rows

        @pl.when(edge > start // rows)
        def _():
            before_edge[edge] = edge * rows - start
            after_edge[edge] = end - edge * rows

        return end

    lax.fori_loop(0, lengths.shape[0], place, 0)

    entry = lax.broadcasted_iota(jnp.int32, (8, 128), 1)
    down_limit = jnp.full((8, 128), -1, jnp.int32)
    up_limit = jnp.full((8, 128), -1, jnp.int32)
    for number, (down, up) in enumerate(menu):
        down_limit = jnp.where(entry == number, levels[down], down_limit)
        up_limit = jnp.where(entry == number, levels[up], up_limit)

    def check(edge, fits):
        after = round_up(after_edge[edge])
        before = round_up(before_edge[edge])
        taken = jnp.zeros((8, 128), jnp.int32)
        for count in range(1, heads + 1):
            taken += jnp.where(after * count <= down_limit, 1, 0)
            taken += jnp.where(before * count <= up_limit, 1, 0)
        return jnp.minimum(fits, jnp.where(taken >= heads, 1, 0))

    fits = lax.fori_loop(1, blocks, check, jnp.ones((8, 128), jnp.int32))
    chosen = jnp.min(jnp.where(fits == 1, entry, len(menu) - 1))
    down_level = jnp.int32(len(levels) - 1)
    up_level = jnp.int32(len(levels) - 1)
    down_rows = jnp.int32(levels[-1])
    up_rows = jnp.int32(levels[-1])
    for number, (down, up) in enumerate(menu[:-1]):
        down_level = jnp.where(chosen == number, down, down_level)
        up_level = jnp.where(chosen == number, up, up_level)
        down_rows = jnp.where(chosen == number, levels[down], down_rows)
        up_rows = jnp.where(chosen == number, levels[up], up_rows)
    down_choice[0] = down_level
    up_choice[0] = up_level
    plan[DOWN_LEVEL] = down_level
    plan[UP_LEVEL] = up_level

    block = lax.axis_index("dp")
    for field, edge in ((A_BELOW, block), (A_ABOVE, block + 1)):
        before = before_edge[edge]
        after = after_edge[edge]
        most = jnp.int32(0)
        least = jnp.int32(heads)
        for count in range(1, heads + 1):
            most += jnp.where(round_up(after) * count <= down_rows, 1, 0)
            least -= jnp.where(round_up(before) * count <= up_rows, 1, 0)
        low = jnp.clip(jnp.int32(heads // 2), least, most)
        plan[field] = before
        plan[field + 1] = after
        plan[field + 2] = jnp.where(before > 0, low, 0)
        plan[field + 3] = jnp.where(before > 0, heads - low, 0)


def tiles(start, size):
    return pl.ds(pl.multiple_of(start, TILE), pl.multiple_of(size, TILE))


def lanes(head):
    return pl.ds(pl.multiple_of(head * HEAD_DIM, HEAD_DIM), HEAD_DIM)


def attention(query, key, value, grad, mask_columns, store, chunk):
    count = query.shape[0]
    key_t = key.T
    value_t = value.T
    across = (((1,), (1,)), ((), ()))
    chunks = [slice(first, first + chunk) for first in range(0, count, chunk)]
    scores = [
        lax.dot_general(key, query[cols], across, preferred_element_type=jnp.float32)
        for cols in chunks
    ]
    grad_probs = [
        lax.dot_general(value, grad[cols], across, preferred_element_type=jnp.float32)
        for cols in chunks
    ]
    probs_low = []
    grad_scores = []
    for number, cols in enumerate(chunks):
        masked = jnp.where(mask_columns(cols), scores[number], -1e30)
        top = jnp.max(masked, axis=0, keepdims=True)
        weights = jnp.exp2((masked - top) * (FACTOR * LOG2E))
        total = jnp.sum(weights, axis=0, keepdims=True)
        probs = weights * (1.0 / total)
        probs_low.append(probs.astype(jnp.bfloat16))
        result_t = jnp.dot(value_t, probs_low[-1], preferred_element_type=jnp.float32)
        weighted = probs * grad_probs[number]
        centre = jnp.sum(weighted, axis=0, keepdims=True)
        grad_scores.append((weighted - probs * centre).astype(jnp.bfloat16))
        grad_query_t = jnp.dot(key_t, grad_scores[-1], preferred_element_type=jnp.float32) * FACTOR
        store(0, cols, result_t.astype(jnp.bfloat16).T)
        store(1, cols, grad_query_t.astype(jnp.bfloat16).T)
    probs_low = jnp.concatenate(probs_low, axis=1)
    grad_scores = jnp.concatenate(grad_scores, axis=1)
    grad_value = jnp.dot(probs_low, grad, preferred_element_type=jnp.float32)
    store(3, slice(None), grad_value.astype(jnp.bfloat16))
    grad_key = jnp.dot(grad_scores, query, preferred_element_type=jnp.float32)
    store(2, slice(None), (grad_key * FACTOR).astype(jnp.bfloat16))


def local_kernel(lengths, query_ref, key_ref, value_ref, grad_ref, *rest):
    outs = rest[:4]
    image_rows = rest[4]
    count = query_ref.shape[0]

    @pl.when(pl.program_id(0) == 0)
    def _():
        position = lax.axis_index("dp") * count + lax.broadcasted_iota(jnp.int32, (8, count), 1)

        def place(image, carry):
            start, begin = carry
            return start + lengths[image], jnp.where(position >= start, start, begin)

        first = (jnp.int32(0), jnp.zeros((8, count), jnp.int32))
        _, begin = lax.fori_loop(0, lengths.shape[0], place, first)
        image_rows[...] = begin.astype(jnp.float32)

    image_col = image_rows[...].T[:, :1]

    def store(which, rows, part):
        outs[which][rows, :] = part

    attention(
        query_ref[...],
        key_ref[...],
        value_ref[...],
        grad_ref[...],
        lambda cols: image_col == image_rows[:1, cols],
        store,
        LOCAL_CHUNK,
    )


def local_attention(lengths, arrays):
    rows, width = arrays[0].shape
    heads = width // HEAD_DIM
    block = pl.BlockSpec((rows, HEAD_DIM), lambda head: (0, head))
    return pl.pallas_call(
        local_kernel,
        grid=(heads,),
        in_specs=[pl.BlockSpec(memory_space=pltpu.SMEM)] + [block] * 4,
        out_specs=[block] * 4,
        out_shape=[jax.ShapeDtypeStruct((rows, width), jnp.bfloat16)] * 4,
        scratch_shapes=[pltpu.VMEM((8, rows), jnp.float32)],
        compiler_params=pltpu.CompilerParams(vmem_limit_bytes=VMEM_LIMIT),
        cost_estimate=pl.CostEstimate(
            flops=12 * rows * rows * width, bytes_accessed=16 * rows * width, transcendentals=0
        ),
        name="local_images",
    )(lengths, *arrays)


START = lambda copy: copy.start()
WAIT = lambda copy: copy.wait()


def pieces(levels):
    starts = (0,) + levels[:-1]
    return [(start, end - start) for start, end in zip(starts, levels)]


def copy_pieces(levels, level, staged, offset, arrays, sems, out, action):
    for number, (start, size) in enumerate(pieces(levels)):
        inside = staged.at[pl.ds(offset + start, size)]
        outside = arrays[number]
        source, target = (inside, outside) if out else (outside, inside)

        @pl.when(True if number == 0 else level >= number)
        def _():
            action(pltpu.make_async_copy(source, target, sems.at[number]))


def pack_kernel(levels, blocks, lengths, query, key, value, grad, *rest):
    count = len(levels)
    plan, down_choice, up_choice = rest[:3]
    down, up = rest[3:3 + count], rest[3 + count:3 + 2 * count]
    before_edge, after_edge, held, down_staged, up_staged, sems, down_sem, up_sem = rest[
        3 + 2 * count:]
    rows, width = query.shape
    heads = width // HEAD_DIM
    loads = [
        pltpu.make_async_copy(array, held.at[which, pl.ds(0, rows)], sems.at[which])
        for which, array in enumerate((query, key, value, grad))
    ]
    for copy in loads:
        copy.start()
    make_plan(
        heads, rows, blocks, levels, lengths, plan, down_choice, up_choice,
        before_edge, after_edge)
    after = round_up(plan[C_BELOW])
    before = round_up(plan[A_ABOVE])
    to_lower = plan[HERE_BELOW]
    to_upper = plan[THERE_ABOVE]

    def gather(staged, count, first_head, taken, first_row):
        steps = (taken + BLOCK - 1) // BLOCK

        def one_head(slot, carry):
            def one_block(step, carry):
                source = pl.ds(pl.multiple_of(first_row + step * BLOCK, TILE), BLOCK)
                target = pl.ds(pl.multiple_of(slot * taken + step * BLOCK, TILE), BLOCK)
                for which in range(4):
                    staged[target, which * HEAD_DIM:(which + 1) * HEAD_DIM] = held[
                        which, source, lanes(first_head + slot)]
                return carry

            return lax.fori_loop(0, steps, one_block, carry)

        lax.fori_loop(0, count, one_head, 0)

    for copy in loads:
        copy.wait()
    gather(down_staged, to_lower, 0, after, 0)
    move_down = functools.partial(
        copy_pieces, levels, plan[DOWN_LEVEL], down_staged, 0, down, down_sem, True)
    move_down(START)
    gather(up_staged, to_upper, heads - to_upper, before, rows - before)
    move_up = functools.partial(
        copy_pieces, levels, plan[UP_LEVEL], up_staged, 0, up, up_sem, True)
    move_up(START)
    move_down(WAIT)
    move_up(WAIT)


def piece_shapes(levels):
    return [jax.ShapeDtypeStruct((size, 4 * HEAD_DIM), jnp.bfloat16) for _, size in pieces(levels)]


def pack(lengths, arrays, levels, blocks):
    rows, width = arrays[0].shape
    count = len(levels)
    anywhere = pl.BlockSpec(memory_space=pl.ANY)
    scalars = pl.BlockSpec(memory_space=pltpu.SMEM)
    staged = pltpu.VMEM((levels[-1] + BLOCK, 4 * HEAD_DIM), jnp.bfloat16)
    plan, down_choice, up_choice, *outs = pl.pallas_call(
        functools.partial(pack_kernel, levels, blocks),
        in_specs=[scalars] + [anywhere] * 4,
        out_specs=[scalars] * 3 + [anywhere] * (2 * count),
        out_shape=[
            jax.ShapeDtypeStruct((UP_LEVEL + 1,), jnp.int32),
            jax.ShapeDtypeStruct((1,), jnp.int32),
            jax.ShapeDtypeStruct((1,), jnp.int32),
        ] + piece_shapes(levels) * 2,
        scratch_shapes=[
            pltpu.SMEM((blocks + 1,), jnp.int32),
            pltpu.SMEM((blocks + 1,), jnp.int32),
            pltpu.VMEM((4, rows + BLOCK, width), jnp.bfloat16),
            staged,
            staged,
            pltpu.SemaphoreType.DMA((4,)),
            pltpu.SemaphoreType.DMA((count,)),
            pltpu.SemaphoreType.DMA((count,)),
        ],
        compiler_params=pltpu.CompilerParams(vmem_limit_bytes=PACK_VMEM_LIMIT),
        name="pack",
    )(lengths, *arrays)
    return plan, down_choice, up_choice, outs[:count], outs[count:]


def crossing_kernel(levels, above, plan, query, key, value, grad, *rest):
    count = len(levels)
    received, back, kept = rest[:count], rest[count:2 * count], rest[2 * count]
    own, staged_in, staged_out, result, own_sem, in_sem, out_sem, kept_sem = rest[2 * count + 1:]
    rows, width = query.shape
    heads = width // HEAD_DIM
    jobs = plan[HERE_ABOVE] if above else plan[THERE_BELOW]
    before = plan[A_ABOVE] if above else plan[A_BELOW]
    after = plan[C_ABOVE] if above else plan[C_BELOW]
    first_head = 0 if above else heads - jobs
    if above:
        own_part = tiles(rows - round_up(before), round_up(before))
        moved_rows = round_up(after)
        margin = 0
        shift = 0
    else:
        own_part = tiles(0, round_up(after))
        moved_rows = round_up(before)
        margin = rows
        shift = moved_rows

    def load_own(action):
        for which, array in enumerate((query, key, value, grad)):
            action(pltpu.make_async_copy(
                array.at[own_part], own.at[which, own_part], own_sem.at[which]))

    def keep(job):
        buffer = lax.rem(job, 2)
        return pltpu.make_async_copy(
            result.at[buffer, own_part], kept.at[job, own_part], kept_sem.at[buffer])

    position = lax.broadcasted_iota(jnp.int32, (rows, HEAD_DIM), 0)
    in_first = position < after
    in_last = position >= rows - before
    in_moved, in_own = (in_first, in_last) if above else (in_last, in_first)
    key_position = lax.broadcasted_iota(jnp.int32, (rows, 1), 0)
    in_image = (key_position < after) | (key_position >= rows - before)

    def one_job(step, carry):
        job = step if above else jobs - 1 - step
        buffer = lax.rem(job, 2)
        window = pl.ds(pl.multiple_of(job * moved_rows + shift, TILE), rows)

        @pl.when(step >= 2)
        def _():
            keep(job).wait()

        zero = jnp.zeros((rows, HEAD_DIM), jnp.bfloat16)
        operands = []
        for which in range(4):
            columns = slice(which * HEAD_DIM, (which + 1) * HEAD_DIM)
            operands.append(jnp.where(
                in_moved,
                staged_in[window, columns],
                jnp.where(in_own, own[which, :, lanes(first_head + job)], zero),
            ))

        def store(which, part_rows, part):
            result[buffer, part_rows, which * HEAD_DIM:(which + 1) * HEAD_DIM] = part

        attention(*operands, lambda cols: in_image, store, CROSSING_CHUNK)
        staged_out[window, :] = result[buffer]
        keep(job).start()
        return carry

    @pl.when(jobs > 0)
    def _():
        level = plan[DOWN_LEVEL] if above else plan[UP_LEVEL]
        stage = functools.partial(
            copy_pieces, levels, level, staged_in, margin, received, in_sem, False)
        send = functools.partial(
            copy_pieces, levels, level, staged_out, margin, back, out_sem, True)
        stage(START)
        load_own(START)
        load_own(WAIT)
        stage(WAIT)
        lax.fori_loop(0, jobs, one_job, 0)
        send(START)

        @pl.when(jobs >= 2)
        def _():
            keep(jobs - 2 if above else 1).wait()

        keep(jobs - 1 if above else 0).wait()
        send(WAIT)


def crossing_images(above, plan, arrays, received, levels):
    rows, width = arrays[0].shape
    heads = width // HEAD_DIM
    four = 4 * HEAD_DIM
    count = len(levels)
    anywhere = pl.BlockSpec(memory_space=pl.ANY)
    staged = pltpu.VMEM((levels[-1] + rows, four), jnp.bfloat16)
    outs = pl.pallas_call(
        functools.partial(crossing_kernel, levels, above),
        in_specs=[pl.BlockSpec(memory_space=pltpu.SMEM)] + [anywhere] * (4 + count),
        out_specs=[anywhere] * (count + 1),
        out_shape=piece_shapes(levels)
        + [jax.ShapeDtypeStruct((heads, rows, four), jnp.bfloat16)],
        scratch_shapes=[
            pltpu.VMEM((4, rows, width), jnp.bfloat16),
            staged,
            staged,
            pltpu.VMEM((2, rows, four), jnp.bfloat16),
            pltpu.SemaphoreType.DMA((4,)),
            pltpu.SemaphoreType.DMA((count,)),
            pltpu.SemaphoreType.DMA((count,)),
            pltpu.SemaphoreType.DMA((2,)),
        ],
        compiler_params=pltpu.CompilerParams(vmem_limit_bytes=VMEM_LIMIT),
        name="above_images" if above else "below_images",
    )(plan, *arrays, *received)
    return outs[:count], outs[count]


def overlay(whole, which, first_head, last_head, first_block, last_block, wanted, source):
    def one_head(head, carry):
        def one_block(block, carry):
            part = pl.ds(pl.multiple_of(block * BLOCK, BLOCK), BLOCK)
            position = block * BLOCK + lax.broadcasted_iota(jnp.int32, (BLOCK, HEAD_DIM), 0)
            whole[which, part, lanes(head)] = jnp.where(
                wanted(position), source(head, block), whole[which, part, lanes(head)])
            return carry

        return lax.fori_loop(first_block, last_block, one_block, carry)

    lax.fori_loop(first_head, last_head, one_head, 0)


def block_part(block):
    return pl.ds(pl.multiple_of(block * BLOCK, BLOCK), BLOCK)


def most_kernel(levels, plan, kept_above, kept_below, *rest):
    count = len(levels)
    from_below, local, outs = rest[:count], rest[count:count + 4], rest[count + 4:count + 8]
    (whole, first_part, last_part, below_staged, whole_sem, first_sem, last_sem, below_sem,
     out_sem) = rest[count + 8:]
    rows, width = local[0].shape
    heads = width // HEAD_DIM
    low_below = plan[HERE_BELOW]
    low_above = plan[HERE_ABOVE]
    below_jobs = plan[THERE_BELOW]
    after = plan[C_BELOW]
    begin = rows - plan[A_ABOVE]
    after_rows = round_up(after)
    first_tiles = tiles(0, after_rows)
    last_tiles = tiles(rows - round_up(plan[A_ABOVE]), round_up(plan[A_ABOVE]))

    def parts(action):
        for slot in range(heads):
            @pl.when(slot < below_jobs)
            def _():
                action(pltpu.make_async_copy(
                    kept_below.at[slot, first_tiles], first_part.at[slot, first_tiles],
                    first_sem.at[slot]))

            @pl.when(slot < low_above)
            def _():
                action(pltpu.make_async_copy(
                    kept_above.at[slot, last_tiles], last_part.at[slot, last_tiles],
                    last_sem.at[slot]))

    loads = [
        pltpu.make_async_copy(local[which], whole.at[which], whole_sem.at[which])
        for which in range(4)
    ]
    saves = [
        pltpu.make_async_copy(whole.at[which], outs[which], out_sem.at[which])
        for which in range(4)
    ]
    stage = functools.partial(
        copy_pieces, levels, plan[DOWN_LEVEL], below_staged, 0, from_below, below_sem, False)
    parts(START)
    stage(START)
    for copy in loads:
        copy.start()
    parts(WAIT)
    stage(WAIT)
    for which in range(4):
        columns = slice(which * HEAD_DIM, (which + 1) * HEAD_DIM)

        def moved_source(head, block):
            start = pl.multiple_of(head * after_rows + block * BLOCK, TILE)
            return below_staged[pl.ds(start, BLOCK), columns]

        def kept_source(head, block):
            return first_part[head - low_below, block_part(block), columns]

        def last_source(head, block):
            return last_part[head, block_part(block), columns]

        in_first = lambda position: position < after
        first_blocks = (0, (after + BLOCK - 1) // BLOCK)
        loads[which].wait()
        overlay(whole, which, 0, low_below, *first_blocks, in_first, moved_source)
        overlay(whole, which, low_below, low_below + below_jobs, *first_blocks, in_first,
                kept_source)
        overlay(whole, which, 0, low_above, begin // BLOCK, rows // BLOCK,
                lambda position: position >= begin, last_source)
        saves[which].start()
    for copy in saves:
        copy.wait()


def merge_most(plan, kept_above, kept_below, from_below, local, levels):
    rows, width = local[0].shape
    heads = width // HEAD_DIM
    four = 4 * HEAD_DIM
    count = len(levels)
    anywhere = pl.BlockSpec(memory_space=pl.ANY)
    windows = pltpu.VMEM((heads, rows, four), jnp.bfloat16)
    return pl.pallas_call(
        functools.partial(most_kernel, levels),
        in_specs=[pl.BlockSpec(memory_space=pltpu.SMEM)] + [anywhere] * (6 + count),
        out_specs=[anywhere] * 4,
        out_shape=[jax.ShapeDtypeStruct((rows, width), jnp.bfloat16)] * 4,
        scratch_shapes=[
            pltpu.VMEM((4, rows, width), jnp.bfloat16),
            windows,
            windows,
            pltpu.VMEM((levels[-1] + BLOCK, four), jnp.bfloat16),
            pltpu.SemaphoreType.DMA((4,)),
            pltpu.SemaphoreType.DMA((heads,)),
            pltpu.SemaphoreType.DMA((heads,)),
            pltpu.SemaphoreType.DMA((count,)),
            pltpu.SemaphoreType.DMA((4,)),
        ],
        compiler_params=pltpu.CompilerParams(vmem_limit_bytes=VMEM_LIMIT),
        cost_estimate=pl.CostEstimate(
            flops=0, bytes_accessed=32 * rows * width, transcendentals=0
        ),
        name="merge_most",
    )(plan, kept_above, kept_below, *from_below, *local)


def last_kernel(levels, plan, *rest):
    count = len(levels)
    from_above = rest[:count]
    outs = rest[count + 4:count + 8]
    whole, staged, whole_sem, staged_sem = rest[count + 8:]
    rows = whole.shape[1]
    heads = whole.shape[2] // HEAD_DIM
    before = plan[A_ABOVE]
    before_rows = round_up(before)
    moved = plan[THERE_ABOVE]
    begin = rows - before
    first_block = begin // BLOCK
    part = pl.ds(
        pl.multiple_of(first_block * BLOCK, BLOCK),
        pl.multiple_of(rows - first_block * BLOCK, BLOCK))

    def move(which, out):
        inside, outside = whole.at[which, part], outs[which].at[part]
        source, target = (inside, outside) if out else (outside, inside)
        return pltpu.make_async_copy(source, target, whole_sem.at[which])

    stage = functools.partial(
        copy_pieces, levels, plan[UP_LEVEL], staged, BLOCK, from_above, staged_sem, False)

    @pl.when(moved > 0)
    def _():
        stage(START)
        for which in range(4):
            move(which, False).start()
        stage(WAIT)
        for which in range(4):
            columns = slice(which * HEAD_DIM, (which + 1) * HEAD_DIM)

            def source(head, block):
                slot = head - (heads - moved)
                start = BLOCK + slot * before_rows + block * BLOCK - (rows - before_rows)
                return staged[pl.ds(pl.multiple_of(start, TILE), BLOCK), columns]

            move(which, False).wait()
            overlay(whole, which, heads - moved, heads, first_block, rows // BLOCK,
                    lambda position: position >= begin, source)
            move(which, True).start()
        for which in range(4):
            move(which, True).wait()


def merge_last(plan, from_above, outs, levels):
    rows, width = outs[0].shape
    count = len(levels)
    anywhere = pl.BlockSpec(memory_space=pl.ANY)
    return pl.pallas_call(
        functools.partial(last_kernel, levels),
        in_specs=[pl.BlockSpec(memory_space=pltpu.SMEM)] + [anywhere] * (count + 4),
        out_specs=[anywhere] * 4,
        out_shape=[jax.ShapeDtypeStruct((rows, width), jnp.bfloat16)] * 4,
        input_output_aliases={1 + count + which: which for which in range(4)},
        scratch_shapes=[
            pltpu.VMEM((4, rows, width), jnp.bfloat16),
            pltpu.VMEM((levels[-1] + 2 * BLOCK, 4 * HEAD_DIM), jnp.bfloat16),
            pltpu.SemaphoreType.DMA((4,)),
            pltpu.SemaphoreType.DMA((count,)),
        ],
        compiler_params=pltpu.CompilerParams(vmem_limit_bytes=VMEM_LIMIT),
        name="merge_last",
    )(plan, *from_above, *outs)


def passed_along(value, steps):
    count = lax.axis_size("dp")
    leading, last = max(0, -steps), min(count, count - steps)
    return lax.ppermute(value, "dp", [(source, source + steps) for source in range(leading, last)])


def pass_further(level, arrays, steps):
    if not arrays:
        return []

    def send(used, arrays):
        return [
            passed_along(array, steps) if number < used else jnp.zeros_like(array)
            for number, array in enumerate(arrays)
        ]

    branches = [functools.partial(send, used) for used in range(len(arrays) + 1)]
    return lax.switch(level[0], branches, list(arrays))


def body(queries, keys, values, out_grad, lengths):
    rows, width = queries.shape
    arrays = (queries, keys, values, out_grad)
    levels = size_levels(rows, width // HEAD_DIM)
    plan, down_level, up_level, down, up = pack(lengths, arrays, levels, lax.axis_size("dp"))
    from_above = passed_along(down[0], -1)
    local = local_attention(lengths, arrays)
    up_first, down_level, local = lax.optimization_barrier((up[0], down_level, local))
    from_below = passed_along(up_first, 1)
    from_above = [from_above, *pass_further(down_level, down[1:], -1)]
    back_up, kept_above = crossing_images(True, plan, arrays, from_above, levels)
    back_below = passed_along(back_up[0], 1)
    up_level, kept_above = lax.optimization_barrier((up_level, kept_above))
    from_below = [from_below, *pass_further(up_level, up[1:], 1)]
    back_down, kept_below = crossing_images(False, plan, arrays, from_below, levels)
    back_above = passed_along(back_down[0], -1)
    down_level, kept_below = lax.optimization_barrier((down_level, kept_below))
    back_below = [back_below, *pass_further(down_level, back_up[1:], 1)]
    outs = merge_most(plan, kept_above, kept_below, back_below, local, levels)
    up_level, outs = lax.optimization_barrier((up_level, outs))
    back_above = [back_above, *pass_further(up_level, back_down[1:], -1)]
    return tuple(merge_last(plan, back_above, outs, levels))


def solution(mesh):
    in_specs = (P("dp", "tensor"), P("dp", "tensor"), P("dp", "tensor"), P("dp", "tensor"), P())
    out_specs = (P("dp", "tensor"), P("dp", "tensor"), P("dp", "tensor"), P("dp", "tensor"))
    return jax.shard_map(body, mesh=mesh, in_specs=in_specs, out_specs=out_specs, check_vma=False)
```

profile of v0, /device:TPU:14, one launch (start us, length us, event | category | flops | bytes accessed | tf_op | source)
XLA Modules:
  0.0 108.7 jit_solution(10542654884715331898)
XLA Ops:
  0.6 0.0 copy-start.3
  0.6 0.0 copy-start.2
  0.7 0.0 copy-start.1
  0.7 0.0 copy-start
  0.7 0.0 copy-start.5
  0.7 4.7 %pack.1 = (s32[10]{0:T(128)}, s32[1]{0:T(128)}, s32[1]{0:T(128)}, bf16[896,512]{1,0:T(8,128)(2,1)}, bf16[896,512]{1,0:T(8,128)(2,1)}) custom-call(s32[32]{0:T(128)} %lengths.3, bf16[512,768]{1,0:T(8,128)(2,1)} %query.5, bf16[512,768]{1,0:T(8,128)(2,1)} %key.5, bf16[512,768]{1,0:T(8,128)(2,1)} %value.5, bf16[512,768]{1,0:T(8,128)(2,1)} %grad.5), custom_call_target="tpu_custom_call" | custom-call | tf_op jit(solution)/shard_map/pack/pallas_call | solution.py:303
  5.4 0.0 copy-start.6
  5.4 0.0 copy-start.4
  5.5 2.6 %collective-permute-start.2 = (bf16[896,512]{1,0:T(8,128)(2,1)}, bf16[896,512]{1,0:T(8,128)(2,1)S(1)}, u32[]{:S(2)}, u32[]{:S(2)}) collective-permute-start(bf16[896,512]{1,0:T(8,128)(2,1)} %get-tuple-element.32), channel_id=1, source_target_pairs={{4,0},{8,4},{12,8},{16,12},{20,16},{24,20},{28,24},{5,1},{9,5},{13... | collective-permute-start | bytes 2752520 | tf_op jit(solution)/shard_map/ppermute | solution.py:635
  8.0 0.0 copy-done.3
  8.0 0.0 copy-done.2
  8.0 0.0 copy-done.1
  8.1 0.0 copy-done
  8.1 0.0 copy-done.5
  8.1 9.6 %local_images.1 = (bf16[512,768]{1,0:T(8,128)(2,1)S(1)}, bf16[512,768]{1,0:T(8,128)(2,1)S(1)}, bf16[512,768]{1,0:T(8,128)(2,1)S(1)}, bf16[512,768]{1,0:T(8,128)(2,1)S(1)}) custom-call(s32[32]{0:T(128)S(1)} %copy-done.5, bf16[512,768]{1,0:T(8,128)(2,1)S(1)} %copy-done, bf16[512,768]{1,0:T(8,128)(2,1)S(1)} %copy-done.1, bf16[512,768]{1,0:T(8,128)(2,1)S(1)} %copy-done.2, ...), custom_call_target="tpu_custom_call" | custom-call | flops 2415919104 | bytes 6291456 | tf_op jit(solution)/shard_map/local_images/pallas_call | solution.py:206
  17.7 0.0 copy-done.6
  17.7 4.3 %collective-permute-start = (bf16[896,512]{1,0:T(8,128)(2,1)S(1)}, bf16[896,512]{1,0:T(8,128)(2,1)S(1)}, u32[]{:S(2)}, u32[]{:S(2)}) collective-permute-start(bf16[896,512]{1,0:T(8,128)(2,1)S(1)} %copy-done.6), channel_id=1, source_target_pairs={{0,4},{4,8},{8,12},{12,16},{16,20},{20,24},{24,28},{1,5},{5,9},{9,... | collective-permute-start | bytes 2752520 | tf_op jit(solution)/shard_map/ppermute | solution.py:635
  22.0 25.6 %collective-permute-done.2.rest_0_ = bf16[896,512]{1,0:T(8,128)(2,1)S(1)} collective-permute-done((bf16[896,512]{1,0:T(8,128)(2,1)}, bf16[896,512]{1,0:T(8,128)(2,1)S(1)}, u32[]{:S(2)}, u32[]{:S(2)}) %collective-permute-start.2) | collective-permute-done | bytes 917536 | tf_op jit(solution)/shard_map/ppermute | solution.py:635
  47.6 0.0 copy-done.4
  47.6 8.9 %above_images.1 = (bf16[896,512]{1,0:T(8,128)(2,1)S(1)}, bf16[6,512,512]{2,1,0:T(8,128)(2,1)S(1)}) custom-call(s32[10]{0:T(128)S(1)} %copy-done.4, bf16[512,768]{1,0:T(8,128)(2,1)S(1)} %copy-done, bf16[512,768]{1,0:T(8,128)(2,1)S(1)} %copy-done.1, bf16[512,768]{1,0:T(8,128)(2,1)S(1)} %copy-done.2, bf16[512,768]{1,0:T(8,128)(2,1)S(1)} %copy-done.3, ...), custom_call_target="tpu_custom_call" | custom-call | tf_op jit(solution)/shard_map/above_images/pallas_call | solution.py:422
  56.5 2.5 %collective-permute-start.3 = (bf16[896,512]{1,0:T(8,128)(2,1)S(1)}, bf16[896,512]{1,0:T(8,128)(2,1)S(1)}, u32[]{:S(2)}, u32[]{:S(2)}) collective-permute-start(bf16[896,512]{1,0:T(8,128)(2,1)S(1)} %get-tuple-element.35), channel_id=1, source_target_pairs={{0,4},{4,8},{8,12},{12,16},{16,20},{20,24},{24,28},{1,5},{5,9},{9,... | collective-permute-start | bytes 2752520 | tf_op jit(solution)/shard_map/ppermute | solution.py:635
  59.0 0.0 collective-permute-done.rest_0_
  59.0 6.7 %below_images.1 = (bf16[896,512]{1,0:T(8,128)(2,1)S(1)}, bf16[6,512,512]{2,1,0:T(8,128)(2,1)S(1)}) custom-call(s32[10]{0:T(128)S(1)} %copy-done.4, bf16[512,768]{1,0:T(8,128)(2,1)S(1)} %copy-done, bf16[512,768]{1,0:T(8,128)(2,1)S(1)} %copy-done.1, bf16[512,768]{1,0:T(8,128)(2,1)S(1)} %copy-done.2, bf16[512,768]{1,0:T(8,128)(2,1)S(1)} %copy-done.3, ...), custom_call_target="tpu_custom_call" | custom-call | tf_op jit(solution)/shard_map/below_images/pallas_call | solution.py:422
  65.8 7.9 %collective-permute-start.1 = (bf16[896,512]{1,0:T(8,128)(2,1)S(1)}, bf16[896,512]{1,0:T(8,128)(2,1)S(1)}, u32[]{:S(2)}, u32[]{:S(2)}) collective-permute-start(bf16[896,512]{1,0:T(8,128)(2,1)S(1)} %get-tuple-element.31), channel_id=1, source_target_pairs={{4,0},{8,4},{12,8},{16,12},{20,16},{24,20},{28,24},{5,1},{9,5},{13... | collective-permute-start | bytes 2752520 | tf_op jit(solution)/shard_map/ppermute | solution.py:635
  73.6 25.6 %collective-permute-done.3.rest_0_ = bf16[896,512]{1,0:T(8,128)(2,1)S(1)} collective-permute-done((bf16[896,512]{1,0:T(8,128)(2,1)S(1)}, bf16[896,512]{1,0:T(8,128)(2,1)S(1)}, u32[]{:S(2)}, u32[]{:S(2)}) %collective-permute-start.3) | collective-permute-done | bytes 917536 | tf_op jit(solution)/shard_map/ppermute | solution.py:635
  99.2 5.8 %merge_most.1 = (bf16[512,768]{1,0:T(8,128)(2,1)}, bf16[512,768]{1,0:T(8,128)(2,1)}, bf16[512,768]{1,0:T(8,128)(2,1)}, bf16[512,768]{1,0:T(8,128)(2,1)}) custom-call(s32[10]{0:T(128)S(1)} %copy-done.4, bf16[6,512,512]{2,1,0:T(8,128)(2,1)S(1)} %get-tuple-element.33.kept_above, bf16[6,512,512]{2,1,0:T(8,128)(2,1)S(1)} %get-tuple-element.34.kept_below, ...), custom_call_target="tpu_custom_call" | custom-call | bytes 12582912 | tf_op jit(solution)/shard_map/merge_most/pallas_call | solution.py:541
  105.1 0.0 collective-permute-done.1.rest_0_
  105.1 3.6 %merge_last.1 = (bf16[512,768]{1,0:T(8,128)(2,1)}, bf16[512,768]{1,0:T(8,128)(2,1)}, bf16[512,768]{1,0:T(8,128)(2,1)}, bf16[512,768]{1,0:T(8,128)(2,1)}) custom-call(s32[10]{0:T(128)S(1)} %copy-done.4, bf16[896,512]{1,0:T(8,128)(2,1)S(1)} %collective-permute-done.1.rest_0_, ...), custom_call_target="tpu_custom_call", output_to_operand_aliasing={{0}: (2, {}), {1}: (3, {}), {2}: (4, {}), {3}: (5, {})} | custom-call | tf_op jit(solution)/shard_map/merge_last/pallas_call | solution.py:615
Async XLA Ops:
  0.6 7.4 %copy-start.3 = (bf16[512,768]{1,0:T(8,128)(2,1)S(1)}, bf16[512,768]{1,0:T(8,128)(2,1)}, u32[]{:S(2)}) copy-start(bf16[512,768]{1,0:T(8,128)(2,1)} %grad.5) | copy-start | bytes 2359300
  0.6 7.4 %copy-start.2 = (bf16[512,768]{1,0:T(8,128)(2,1)S(1)}, bf16[512,768]{1,0:T(8,128)(2,1)}, u32[]{:S(2)}) copy-start(bf16[512,768]{1,0:T(8,128)(2,1)} %value.5) | copy-start | bytes 2359300
  0.7 7.4 %copy-start.1 = (bf16[512,768]{1,0:T(8,128)(2,1)S(1)}, bf16[512,768]{1,0:T(8,128)(2,1)}, u32[]{:S(2)}) copy-start(bf16[512,768]{1,0:T(8,128)(2,1)} %key.5) | copy-start | bytes 2359300
  0.7 7.4 %copy-start = (bf16[512,768]{1,0:T(8,128)(2,1)S(1)}, bf16[512,768]{1,0:T(8,128)(2,1)}, u32[]{:S(2)}) copy-start(bf16[512,768]{1,0:T(8,128)(2,1)} %query.5) | copy-start | bytes 2359300
  0.7 7.4 %copy-start.5 = (s32[32]{0:T(128)S(1)}, s32[32]{0:T(128)}, u32[]{:S(2)}) copy-start(s32[32]{0:T(128)} %lengths.3) | copy-start | bytes 388
  5.4 12.3 %copy-start.6 = (bf16[896,512]{1,0:T(8,128)(2,1)S(1)}, bf16[896,512]{1,0:T(8,128)(2,1)}, u32[]{:S(2)}) copy-start(bf16[896,512]{1,0:T(8,128)(2,1)} %get-tuple-element.30) | copy-start | bytes 2752516
  5.4 42.1 %copy-start.4 = (s32[10]{0:T(128)S(1)}, s32[10]{0:T(128)}, u32[]{:S(2)}) copy-start(s32[10]{0:T(128)} %get-tuple-element.24.plan) | copy-start | bytes 124
  5.5 42.1 %collective-permute-start.2 = (bf16[896,512]{1,0:T(8,128)(2,1)}, bf16[896,512]{1,0:T(8,128)(2,1)S(1)}, u32[]{:S(2)}, u32[]{:S(2)}) collective-permute-start(bf16[896,512]{1,0:T(8,128)(2,1)} %get-tuple-element.32), channel_id=1, source_target_pairs={{4,0},{8,4},{12,8},{16,12},{20,16},{24,20},{28,24},{5,1},{9,5},{13... | collective-permute-start | bytes 2752520 | tf_op jit(solution)/shard_map/ppermute | solution.py:635
  17.7 41.3 %collective-permute-start = (bf16[896,512]{1,0:T(8,128)(2,1)S(1)}, bf16[896,512]{1,0:T(8,128)(2,1)S(1)}, u32[]{:S(2)}, u32[]{:S(2)}) collective-permute-start(bf16[896,512]{1,0:T(8,128)(2,1)S(1)} %copy-done.6), channel_id=1, source_target_pairs={{0,4},{4,8},{8,12},{12,16},{16,20},{20,24},{24,28},{1,5},{5,9},{9,... | collective-permute-start | bytes 2752520 | tf_op jit(solution)/shard_map/ppermute | solution.py:635
  56.5 42.8 %collective-permute-start.3 = (bf16[896,512]{1,0:T(8,128)(2,1)S(1)}, bf16[896,512]{1,0:T(8,128)(2,1)S(1)}, u32[]{:S(2)}, u32[]{:S(2)}) collective-permute-start(bf16[896,512]{1,0:T(8,128)(2,1)S(1)} %get-tuple-element.35), channel_id=1, source_target_pairs={{0,4},{4,8},{8,12},{12,16},{16,20},{20,24},{24,28},{1,5},{5,9},{9,... | collective-permute-start | bytes 2752520 | tf_op jit(solution)/shard_map/ppermute | solution.py:635
  65.8 39.3 %collective-permute-start.1 = (bf16[896,512]{1,0:T(8,128)(2,1)S(1)}, bf16[896,512]{1,0:T(8,128)(2,1)S(1)}, u32[]{:S(2)}, u32[]{:S(2)}) collective-permute-start(bf16[896,512]{1,0:T(8,128)(2,1)S(1)} %get-tuple-element.31), channel_id=1, source_target_pairs={{4,0},{8,4},{12,8},{16,12},{20,16},{24,20},{28,24},{5,1},{9,5},{13... | collective-permute-start | bytes 2752520 | tf_op jit(solution)/shard_map/ppermute | solution.py:635
where the time goes:
time: 110 us; the launch traced here: 109 us
  waiting for transfers between devices  51.2 us (47%)
  Pallas kernels  39.4 us (36%)
  starting transfers between devices  17.2 us (16%)
    ppermute x4, waiting for transfers between devices, passed_along(): lax.ppermute(value, 'dp', [(source, source + steps) for source in range(l...  51.2 us
    ppermute x4, starting transfers between devices, passed_along(): lax.ppermute(value, 'dp', [(source, source + steps) for source in range(l...  17.2 us
    pallas_call x2, Pallas kernels, crossing_images(): pl.pallas_call(functools.partial(crossing_kernel, levels, above), in_spec...  15.6 us
    pallas_call x1, Pallas kernels, local_attention(): pl.pallas_call(local_kernel, grid=(heads,), in_specs=[pl.BlockSpec(memory...  9.6 us
    pallas_call x1, Pallas kernels, merge_most(): pl.pallas_call(functools.partial(most_kernel, levels), in_specs=[pl.Block...  5.83 us
    pallas_call x1, Pallas kernels, pack(): pl.pallas_call(functools.partial(pack_kernel, levels, blocks), in_specs=[...  4.74 us
    pallas_call x1, Pallas kernels, merge_last(): pl.pallas_call(functools.partial(last_kernel, levels), in_specs=[pl.Block...  3.61 us
  transfers between devices with their start and end apart: 4, of which 2 were waited for; matrix products, arithmetic and copies ran while one was open for 0% of the time, Pallas kernels for 29%

commit v1 on v0

v1 whole, which is shorter than its diff:
```python
import functools
import math

import jax
import jax.numpy as jnp
from jax import lax
from jax.experimental import pallas as pl
from jax.experimental.pallas import tpu as pltpu
from jax.sharding import PartitionSpec as P

HEAD_DIM = 128
TILE = 16
BLOCK = 64
LOCAL_CHUNK = 256
CROSSING_CHUNK = 512
FACTOR = 1.0 / math.sqrt(HEAD_DIM)
LOG2E = 1.4426950408889634
VMEM_LIMIT = 32 * 1024 * 1024
PACK_VMEM_LIMIT = 60 * 1024 * 1024

FIELDS = 8
BEFORE, AFTER, LOWER, JOBS, JOB_HEAD, SENT, SENT_HEAD, LEVEL = range(FIELDS)
ODD, EVEN = 0, 1

LEVEL_UNITS = ((), ())


def round_up(value):
    return (value + (TILE - 1)) // TILE * TILE


def worst_case_rows(rows, heads):
    worst = 0
    for before in range(TILE, rows + 1, TILE):
        for after in range(TILE, rows + TILE - before + 1, TILE):
            needed = min(max(after * low, before * (heads - low)) for low in range(heads + 1))
            worst = max(worst, needed)
    return worst


def size_levels(kind, rows, heads):
    unit = rows * heads // 48
    most = worst_case_rows(rows, heads)
    below = sorted(level * unit for level in LEVEL_UNITS[kind] if level * unit < most)
    return tuple(below) + (most,)


def make_plan(heads, rows, blocks, levels, lengths, plan, choices, before_edge, after_edge):
    def clear(edge, carry):
        before_edge[edge] = 0
        after_edge[edge] = 0
        return carry

    lax.fori_loop(0, blocks + 1, clear, 0)

    def place(image, start):
        end = start + lengths[image]
        edge = (end - 1) // rows

        @pl.when(edge > start // rows)
        def _():
            before_edge[edge] = edge * rows - start
            after_edge[edge] = end - edge * rows

        return end

    lax.fori_loop(0, lengths.shape[0], place, 0)

    entry = lax.broadcasted_iota(jnp.int32, (8, 128), 1)
    for kind in (ODD, EVEN):
        limit = jnp.full((8, 128), levels[kind][-1], jnp.int32)
        for number, level in enumerate(levels[kind]):
            limit = jnp.where(entry == number, level, limit)

        def check(number, fits):
            edge = 2 * number + (1 if kind == ODD else 2)
            after = round_up(after_edge[edge])
            before = round_up(before_edge[edge])
            taken = jnp.zeros((8, 128), jnp.int32)
            for count in range(1, heads + 1):
                taken += jnp.where(after * count <= limit, 1, 0)
                taken += jnp.where(before * count <= limit, 1, 0)
            return jnp.minimum(fits, jnp.where(taken >= heads, 1, 0))

        last = len(levels[kind]) - 1
        chosen = jnp.int32(last)
        if last:
            edges = (blocks - (0 if kind == ODD else 1)) // 2
            fits = lax.fori_loop(0, edges, check, jnp.ones((8, 128), jnp.int32))
            chosen = jnp.min(jnp.where(fits == 1, entry, last))
        most_rows = jnp.int32(levels[kind][-1])
        for number, level in enumerate(levels[kind][:-1]):
            most_rows = jnp.where(chosen == number, level, most_rows)

        block = lax.axis_index("dp")
        lower = lax.rem(block, 2) == (0 if kind == ODD else 1)
        edge = jnp.where(lower, block + 1, block)
        before = before_edge[edge]
        after = after_edge[edge]
        most = jnp.int32(0)
        least = jnp.int32(heads)
        for count in range(1, heads + 1):
            most += jnp.where(round_up(after) * count <= most_rows, 1, 0)
            least -= jnp.where(round_up(before) * count <= most_rows, 1, 0)
        low = jnp.clip(jnp.int32(heads // 2), least, most)
        crossed = before > 0
        base = kind * FIELDS
        plan[base + BEFORE] = before
        plan[base + AFTER] = after
        plan[base + LOWER] = lower.astype(jnp.int32)
        plan[base + JOBS] = jnp.where(crossed, jnp.where(lower, low, heads - low), 0)
        plan[base + JOB_HEAD] = jnp.where(lower, 0, low)
        plan[base + SENT] = jnp.where(crossed, jnp.where(lower, heads - low, low), 0)
        plan[base + SENT_HEAD] = jnp.where(lower, low, 0)
        plan[base + LEVEL] = chosen
        choices[kind][0] = chosen


class Edge:
    def __init__(self, plan, kind, rows):
        read = lambda field: plan[kind * FIELDS + field]
        self.lower = read(LOWER) == 1
        self.jobs, self.job_head = read(JOBS), read(JOB_HEAD)
        self.sent, self.sent_head = read(SENT), read(SENT_HEAD)
        self.level = read(LEVEL)
        before, after = read(BEFORE), read(AFTER)
        self.before, self.after = before, after
        self.own_begin = jnp.where(self.lower, rows - before, 0)
        self.own_end = jnp.where(self.lower, rows, after)
        self.own_rows = round_up(jnp.where(self.lower, before, after))
        self.other_rows = round_up(jnp.where(self.lower, after, before))
        self.own = jnp.where(self.lower, rows - self.own_rows, 0)
        self.other = jnp.where(self.lower, 0, rows - self.other_rows)
        self.first_block = self.own_begin // BLOCK
        self.last_block = (self.own_end + BLOCK - 1) // BLOCK


def tiles(start, size):
    return pl.ds(pl.multiple_of(start, TILE), pl.multiple_of(size, TILE))


def lanes(head):
    return pl.ds(pl.multiple_of(head * HEAD_DIM, HEAD_DIM), HEAD_DIM)


def attention(query, key, value, grad, mask_columns, store, chunk):
    count = query.shape[0]
    key_t = key.T
    value_t = value.T
    across = (((1,), (1,)), ((), ()))
    chunks = [slice(first, first + chunk) for first in range(0, count, chunk)]
    scores = [
        lax.dot_general(key, query[cols], across, preferred_element_type=jnp.float32)
        for cols in chunks
    ]
    grad_probs = [
        lax.dot_general(value, grad[cols], across, preferred_element_type=jnp.float32)
        for cols in chunks
    ]
    probs_low = []
    grad_scores = []
    for number, cols in enumerate(chunks):
        masked = jnp.where(mask_columns(cols), scores[number], -1e30)
        top = jnp.max(masked, axis=0, keepdims=True)
        weights = jnp.exp2((masked - top) * (FACTOR * LOG2E))
        total = jnp.sum(weights, axis=0, keepdims=True)
        probs = weights * (1.0 / total)
        probs_low.append(probs.astype(jnp.bfloat16))
        result_t = jnp.dot(value_t, probs_low[-1], preferred_element_type=jnp.float32)
        weighted = probs * grad_probs[number]
        centre = jnp.sum(weighted, axis=0, keepdims=True)
        grad_scores.append((weighted - probs * centre).astype(jnp.bfloat16))
        grad_query_t = jnp.dot(key_t, grad_scores[-1], preferred_element_type=jnp.float32) * FACTOR
        store(0, cols, result_t.astype(jnp.bfloat16).T)
        store(1, cols, grad_query_t.astype(jnp.bfloat16).T)
    probs_low = jnp.concatenate(probs_low, axis=1)
    grad_scores = jnp.concatenate(grad_scores, axis=1)
    grad_value = jnp.dot(probs_low, grad, preferred_element_type=jnp.float32)
    store(3, slice(None), grad_value.astype(jnp.bfloat16))
    grad_key = jnp.dot(grad_scores, query, preferred_element_type=jnp.float32)
    store(2, slice(None), (grad_key * FACTOR).astype(jnp.bfloat16))


def local_kernel(lengths, query_ref, key_ref, value_ref, grad_ref, *rest):
    outs = rest[:4]
    image_rows = rest[4]
    count = query_ref.shape[0]

    @pl.when(pl.program_id(0) == 0)
    def _():
        position = lax.axis_index("dp") * count + lax.broadcasted_iota(jnp.int32, (8, count), 1)

        def place(image, carry):
            start, begin = carry
            return start + lengths[image], jnp.where(position >= start, start, begin)

        first = (jnp.int32(0), jnp.zeros((8, count), jnp.int32))
        _, begin = lax.fori_loop(0, lengths.shape[0], place, first)
        image_rows[...] = begin.astype(jnp.float32)

    image_col = image_rows[...].T[:, :1]

    def store(which, rows, part):
        outs[which][rows, :] = part

    attention(
        query_ref[...],
        key_ref[...],
        value_ref[...],
        grad_ref[...],
        lambda cols: image_col == image_rows[:1, cols],
        store,
        LOCAL_CHUNK,
    )


def local_attention(lengths, arrays):
    rows, width = arrays[0].shape
    heads = width // HEAD_DIM
    block = pl.BlockSpec((rows, HEAD_DIM), lambda head: (0, head))
    return pl.pallas_call(
        local_kernel,
        grid=(heads,),
        in_specs=[pl.BlockSpec(memory_space=pltpu.SMEM)] + [block] * 4,
        out_specs=[block] * 4,
        out_shape=[jax.ShapeDtypeStruct((rows, width), jnp.bfloat16)] * 4,
        scratch_shapes=[pltpu.VMEM((8, rows), jnp.float32)],
        compiler_params=pltpu.CompilerParams(vmem_limit_bytes=VMEM_LIMIT),
        cost_estimate=pl.CostEstimate(
            flops=12 * rows * rows * width, bytes_accessed=16 * rows * width, transcendentals=0
        ),
        name="local_images",
    )(lengths, *arrays)


START = lambda copy: copy.start()
WAIT = lambda copy: copy.wait()
ANYWHERE = pl.BlockSpec(memory_space=pl.ANY)
SCALARS = pl.BlockSpec(memory_space=pltpu.SMEM)


def pieces(levels):
    starts = (0,) + levels[:-1]
    return [(start, end - start) for start, end in zip(starts, levels)]


def piece_shapes(levels):
    return [jax.ShapeDtypeStruct((size, 4 * HEAD_DIM), jnp.bfloat16) for _, size in pieces(levels)]


def copy_pieces(levels, level, staged, offset, arrays, sems, out, action):
    for number, (start, size) in enumerate(pieces(levels)):
        inside = staged.at[pl.ds(offset + start, size)]
        outside = arrays[number]
        source, target = (inside, outside) if out else (outside, inside)

        @pl.when(True if number == 0 else level >= number)
        def _():
            action(pltpu.make_async_copy(source, target, sems.at[number]))


def pack_kernel(levels, blocks, lengths, query, key, value, grad, *rest):
    counts = [len(levels[ODD]), len(levels[EVEN])]
    plan, choices, rest = rest[0], rest[1:3], rest[3:]
    outs = rest[:counts[0]], rest[counts[0]:sum(counts)]
    before_edge, after_edge, held, *staged, sems, odd_sem, even_sem = rest[sum(counts):]
    rows, width = query.shape
    heads = width // HEAD_DIM
    loads = [
        pltpu.make_async_copy(array, held.at[which, pl.ds(0, rows)], sems.at[which])
        for which, array in enumerate((query, key, value, grad))
    ]
    for copy in loads:
        copy.start()
    make_plan(heads, rows, blocks, levels, lengths, plan, choices, before_edge, after_edge)

    def gather(edge, staged):
        steps = (edge.own_rows + BLOCK - 1) // BLOCK

        def one_head(slot, carry):
            def one_block(step, carry):
                source = pl.ds(pl.multiple_of(edge.own + step * BLOCK, TILE), BLOCK)
                target = pl.ds(pl.multiple_of(slot * edge.own_rows + step * BLOCK, TILE), BLOCK)
                for which in range(4):
                    staged[target, which * HEAD_DIM:(which + 1) * HEAD_DIM] = held[
                        which, source, lanes(edge.sent_head + slot)]
                return carry

            return lax.fori_loop(0, steps, one_block, carry)

        lax.fori_loop(0, edge.sent, one_head, 0)

    for copy in loads:
        copy.wait()
    moves = []
    for kind, sem in ((EVEN, even_sem), (ODD, odd_sem)):
        edge = Edge(plan, kind, rows)
        gather(edge, staged[kind])
        move = functools.partial(
            copy_pieces, levels[kind], edge.level, staged[kind], 0, outs[kind], sem, True)
        move(START)
        moves.append(move)
    for move in moves:
        move(WAIT)


def pack(lengths, arrays, levels, blocks):
    rows, width = arrays[0].shape
    counts = [len(levels[ODD]), len(levels[EVEN])]
    one = jax.ShapeDtypeStruct((1,), jnp.int32)
    plan, odd_level, even_level, *outs = pl.pallas_call(
        functools.partial(pack_kernel, levels, blocks),
        in_specs=[SCALARS] + [ANYWHERE] * 4,
        out_specs=[SCALARS] * 3 + [ANYWHERE] * sum(counts),
        out_shape=[jax.ShapeDtypeStruct((2 * FIELDS,), jnp.int32), one, one]
        + piece_shapes(levels[ODD]) + piece_shapes(levels[EVEN]),
        scratch_shapes=[
            pltpu.SMEM((blocks + 2,), jnp.int32),
            pltpu.SMEM((blocks + 2,), jnp.int32),
            pltpu.VMEM((4, rows + BLOCK, width), jnp.bfloat16),
            pltpu.VMEM((levels[ODD][-1] + BLOCK, 4 * HEAD_DIM), jnp.bfloat16),
            pltpu.VMEM((levels[EVEN][-1] + BLOCK, 4 * HEAD_DIM), jnp.bfloat16),
            pltpu.SemaphoreType.DMA((4,)),
            pltpu.SemaphoreType.DMA((counts[ODD],)),
            pltpu.SemaphoreType.DMA((counts[EVEN],)),
        ],
        compiler_params=pltpu.CompilerParams(vmem_limit_bytes=PACK_VMEM_LIMIT),
        name="pack",
    )(lengths, *arrays)
    return plan, (odd_level, even_level), (outs[:counts[0]], outs[counts[0]:])


def crossing_kernel(levels, kind, plan, query, key, value, grad, *rest):
    count = len(levels)
    received, back, kept = rest[:count], rest[count:2 * count], rest[2 * count]
    own, staged_in, staged_out, result, own_sem, in_sem, out_sem, kept_sem = rest[2 * count + 1:]
    rows, width = query.shape
    edge = Edge(plan, kind, rows)
    jobs = edge.jobs
    own_part = tiles(edge.own, edge.own_rows)
    margin = rows

    def load_own(action):
        for which, array in enumerate((query, key, value, grad)):
            action(pltpu.make_async_copy(
                array.at[own_part], own.at[which, own_part], own_sem.at[which]))

    def keep(job):
        buffer = lax.rem(job, 2)
        return pltpu.make_async_copy(
            result.at[buffer, own_part], kept.at[job, own_part], kept_sem.at[buffer])

    position = lax.broadcasted_iota(jnp.int32, (rows, HEAD_DIM), 0)
    in_own = (position >= edge.own_begin) & (position < edge.own_end)
    key_position = lax.broadcasted_iota(jnp.int32, (rows, 1), 0)
    in_image = (key_position < edge.after) | (key_position >= rows - edge.before)
    in_window = (position < edge.after) | (position >= rows - edge.before)

    def one_job(step, carry):
        job = jnp.where(edge.lower, step, jobs - 1 - step)
        buffer = lax.rem(job, 2)
        start = margin + job * edge.other_rows - edge.other
        window = pl.ds(pl.multiple_of(start, TILE), rows)

        @pl.when(step >= 2)
        def _():
            keep(job).wait()

        zero = jnp.zeros((rows, HEAD_DIM), jnp.bfloat16)
        operands = []
        for which in range(4):
            columns = slice(which * HEAD_DIM, (which + 1) * HEAD_DIM)
            operands.append(jnp.where(
                in_own,
                own[which, :, lanes(edge.job_head + job)],
                jnp.where(in_window, staged_in[window, columns], zero),
            ))

        def store(which, part_rows, part):
            result[buffer, part_rows, which * HEAD_DIM:(which + 1) * HEAD_DIM] = part

        attention(*operands, lambda cols: in_image, store, CROSSING_CHUNK)
        staged_out[window, :] = result[buffer]
        keep(job).start()
        return carry

    @pl.when(jobs > 0)
    def _():
        stage = functools.partial(
            copy_pieces, levels, edge.level, staged_in, margin, received, in_sem, False)
        send = functools.partial(
            copy_pieces, levels, edge.level, staged_out, margin, back, out_sem, True)
        stage(START)
        load_own(START)
        load_own(WAIT)
        stage(WAIT)
        lax.fori_loop(0, jobs, one_job, 0)
        send(START)

        @pl.when(jobs >= 2)
        def _():
            keep(1).wait()

        keep(0).wait()
        send(WAIT)


def crossing_images(kind, plan, arrays, received, levels):
    rows, width = arrays[0].shape
    heads = width // HEAD_DIM
    four = 4 * HEAD_DIM
    count = len(levels)
    staged = pltpu.VMEM((rows + levels[-1] + rows, four), jnp.bfloat16)
    outs = pl.pallas_call(
        functools.partial(crossing_kernel, levels, kind),
        in_specs=[SCALARS] + [ANYWHERE] * (4 + count),
        out_specs=[ANYWHERE] * (count + 1),
        out_shape=piece_shapes(levels)
        + [jax.ShapeDtypeStruct((heads, rows, four), jnp.bfloat16)],
        scratch_shapes=[
            pltpu.VMEM((4, rows, width), jnp.bfloat16),
            staged,
            staged,
            pltpu.VMEM((2, rows, four), jnp.bfloat16),
            pltpu.SemaphoreType.DMA((4,)),
            pltpu.SemaphoreType.DMA((count,)),
            pltpu.SemaphoreType.DMA((count,)),
            pltpu.SemaphoreType.DMA((2,)),
        ],
        compiler_params=pltpu.CompilerParams(vmem_limit_bytes=VMEM_LIMIT),
        name="odd_edge_images" if kind == ODD else "even_edge_images",
    )(plan, *arrays, *received)
    return outs[:count], outs[count]


def overlay(whole, which, edge, first_head, heads, source):
    def one_head(slot, carry):
        def one_block(block, carry):
            first = block * BLOCK
            part = pl.ds(pl.multiple_of(first, BLOCK), BLOCK)
            position = first + lax.broadcasted_iota(jnp.int32, (BLOCK, HEAD_DIM), 0)
            whole[which, part, lanes(first_head + slot)] = jnp.where(
                (position >= edge.own_begin) & (position < edge.own_end),
                source(slot, first),
                whole[which, part, lanes(first_head + slot)],
            )
            return carry

        return lax.fori_loop(edge.first_block, edge.last_block, one_block, carry)

    lax.fori_loop(0, heads, one_head, 0)


def returned_source(edge, staged, columns):
    def source(slot, first):
        start = BLOCK + slot * edge.own_rows + first - edge.own
        return staged[pl.ds(pl.multiple_of(start, TILE), BLOCK), columns]

    return source


def most_kernel(levels, plan, kept_odd, kept_even, *rest):
    count = len(levels)
    returned, local, outs = rest[:count], rest[count:count + 4], rest[count + 4:count + 8]
    whole, held, staged, whole_sem, held_sem, staged_sem, out_sem = rest[count + 8:]
    rows, width = local[0].shape
    heads = width // HEAD_DIM
    kept = (kept_odd, kept_even)
    edges = [Edge(plan, kind, rows) for kind in (ODD, EVEN)]

    def parts(action):
        for kind in (ODD, EVEN):
            edge = edges[kind]
            part = tiles(edge.own, edge.own_rows)
            for slot in range(heads):
                @pl.when(slot < edge.jobs)
                def _():
                    action(pltpu.make_async_copy(
                        kept[kind].at[slot, part], held.at[kind, slot, part],
                        held_sem.at[kind, slot]))

    loads = [
        pltpu.make_async_copy(local[which], whole.at[which], whole_sem.at[which])
        for which in range(4)
    ]
    saves = [
        pltpu.make_async_copy(whole.at[which], outs[which], out_sem.at[which])
        for which in range(4)
    ]
    stage = functools.partial(
        copy_pieces, levels, edges[EVEN].level, staged, BLOCK, returned, staged_sem, False)
    parts(START)
    stage(START)
    for copy in loads:
        copy.start()
    parts(WAIT)
    stage(WAIT)
    for which in range(4):
        columns = slice(which * HEAD_DIM, (which + 1) * HEAD_DIM)
        loads[which].wait()
        for kind in (ODD, EVEN):
            overlay(
                whole, which, edges[kind], edges[kind].job_head, edges[kind].jobs,
                lambda slot, first: held[
                    kind, slot, pl.ds(pl.multiple_of(first, BLOCK), BLOCK), columns])
        edge = edges[EVEN]
        overlay(whole, which, edge, edge.sent_head, edge.sent,
                returned_source(edge, staged, columns))
        saves[which].start()
    for copy in saves:
        copy.wait()


def merge_most(plan, kept_odd, kept_even, returned, local, levels):
    rows, width = local[0].shape
    heads = width // HEAD_DIM
    four = 4 * HEAD_DIM
    count = len(levels)
    return pl.pallas_call(
        functools.partial(most_kernel, levels),
        in_specs=[SCALARS] + [ANYWHERE] * (6 + count),
        out_specs=[ANYWHERE] * 4,
        out_shape=[jax.ShapeDtypeStruct((rows, width), jnp.bfloat16)] * 4,
        scratch_shapes=[
            pltpu.VMEM((4, rows, width), jnp.bfloat16),
            pltpu.VMEM((2, heads, rows, four), jnp.bfloat16),
            pltpu.VMEM((levels[-1] + 2 * BLOCK, four), jnp.bfloat16),
            pltpu.SemaphoreType.DMA((4,)),
            pltpu.SemaphoreType.DMA((2, heads)),
            pltpu.SemaphoreType.DMA((count,)),
            pltpu.SemaphoreType.DMA((4,)),
        ],
        compiler_params=pltpu.CompilerParams(vmem_limit_bytes=VMEM_LIMIT),
        cost_estimate=pl.CostEstimate(
            flops=0, bytes_accessed=32 * rows * width, transcendentals=0
        ),
        name="merge_most",
    )(plan, kept_odd, kept_even, *returned, *local)


def last_kernel(levels, plan, *rest):
    count = len(levels)
    returned, outs = rest[:count], rest[count + 4:count + 8]
    whole, staged, whole_sem, staged_sem = rest[count + 8:]
    rows = whole.shape[1]
    edge = Edge(plan, ODD, rows)
    part = pl.ds(
        pl.multiple_of(edge.first_block * BLOCK, BLOCK),
        pl.multiple_of((edge.last_block - edge.first_block) * BLOCK, BLOCK))

    def move(which, out):
        inside, outside = whole.at[which, part], outs[which].at[part]
        source, target = (inside, outside) if out else (outside, inside)
        return pltpu.make_async_copy(source, target, whole_sem.at[which])

    stage = functools.partial(
        copy_pieces, levels, edge.level, staged, BLOCK, returned, staged_sem, False)

    @pl.when(edge.sent > 0)
    def _():
        stage(START)
        for which in range(4):
            move(which, False).start()
        stage(WAIT)
        for which in range(4):
            columns = slice(which * HEAD_DIM, (which + 1) * HEAD_DIM)
            move(which, False).wait()
            overlay(whole, which, edge, edge.sent_head, edge.sent,
                    returned_source(edge, staged, columns))
            move(which, True).start()
        for which in range(4):
            move(which, True).wait()


def merge_last(plan, returned, outs, levels):
    rows, width = outs[0].shape
    count = len(levels)
    return pl.pallas_call(
        functools.partial(last_kernel, levels),
        in_specs=[SCALARS] + [ANYWHERE] * (count + 4),
        out_specs=[ANYWHERE] * 4,
        out_shape=[jax.ShapeDtypeStruct((rows, width), jnp.bfloat16)] * 4,
        input_output_aliases={1 + count + which: which for which in range(4)},
        scratch_shapes=[
            pltpu.VMEM((4, rows, width), jnp.bfloat16),
            pltpu.VMEM((levels[-1] + 2 * BLOCK, 4 * HEAD_DIM), jnp.bfloat16),
            pltpu.SemaphoreType.DMA((4,)),
            pltpu.SemaphoreType.DMA((count,)),
        ],
        compiler_params=pltpu.CompilerParams(vmem_limit_bytes=VMEM_LIMIT),
        name="merge_last",
    )(plan, *returned, *outs)


def swapped(value, kind):
    first = 0 if kind == ODD else 1
    pairs = [(block, block + 1) for block in range(first, lax.axis_size("dp") - 1, 2)]
    return lax.ppermute(value, "dp", pairs + [(after, before) for before, after in pairs])


def swap_further(level, arrays, kind):
    if not arrays:
        return []

    def send(used, arrays):
        return [
            swapped(array, kind) if number < used else jnp.zeros_like(array)
            for number, array in enumerate(arrays)
        ]

    branches = [functools.partial(send, used) for used in range(len(arrays) + 1)]
    return lax.switch(level[0], branches, list(arrays))


def body(queries, keys, values, out_grad, lengths):
    rows, width = queries.shape
    arrays = (queries, keys, values, out_grad)
    levels = [size_levels(kind, rows, width // HEAD_DIM) for kind in (ODD, EVEN)]
    plan, (odd_level, even_level), (odd, even) = pack(
        lengths, arrays, levels, lax.axis_size("dp"))
    even_first = swapped(even[0], EVEN)
    odd_first = swapped(odd[0], ODD)
    local = local_attention(lengths, arrays)
    even_first, even_level, local = lax.optimization_barrier((even_first, even_level, local))
    received = [even_first, *swap_further(even_level, even[1:], EVEN)]
    back_even, kept_even = crossing_images(EVEN, plan, arrays, received, levels[EVEN])
    odd_level, kept_even = lax.optimization_barrier((odd_level, kept_even))
    received = [odd_first, *swap_further(odd_level, odd[1:], ODD)]
    first, received = lax.optimization_barrier((back_even[0], received))
    back_first = swapped(first, EVEN)
    back_odd, kept_odd = crossing_images(ODD, plan, arrays, received, levels[ODD])
    odd_first = swapped(back_odd[0], ODD)
    even_level, kept_odd = lax.optimization_barrier((even_level, kept_odd))
    returned = [back_first, *swap_further(even_level, back_even[1:], EVEN)]
    outs = merge_most(plan, kept_odd, kept_even, returned, local, levels[EVEN])
    odd_level, outs = lax.optimization_barrier((odd_level, outs))
    returned = [odd_first, *swap_further(odd_level, back_odd[1:], ODD)]
    return tuple(merge_last(plan, returned, outs, levels[ODD]))


def solution(mesh):
    in_specs = (P("dp", "tensor"), P("dp", "tensor"), P("dp", "tensor"), P("dp", "tensor"), P())
    out_specs = (P("dp", "tensor"), P("dp", "tensor"), P("dp", "tensor"), P("dp", "tensor"))
    return jax.shard_map(body, mesh=mesh, in_specs=in_specs, out_specs=out_specs, check_vma=False)
```

time: 110 us -> 98.9 us (0.90)
  the two profiles are of different devices: /device:TPU:14 before, /device:TPU:26 now
where the time goes in v1:
time: 98.9 us; the launch traced here: 97.4 us
  waiting for transfers between devices  57.3 us (58%)
  Pallas kernels  32.4 us (33%)
  starting transfers between devices  6.87 us (7%)
    ppermute x4, waiting for transfers between devices, swapped(): lax.ppermute(value, 'dp', pairs + [(after, before) for before, after in p...  57.3 us
    pallas_call x2, Pallas kernels, crossing_images(): pl.pallas_call(functools.partial(crossing_kernel, levels, kind), in_specs...  12.1 us
    pallas_call x1, Pallas kernels, local_attention(): pl.pallas_call(local_kernel, grid=(heads,), in_specs=[pl.BlockSpec(memory...  9.6 us
    ppermute x4, starting transfers between devices, swapped(): lax.ppermute(value, 'dp', pairs + [(after, before) for before, after in p...  6.87 us
    pallas_call x1, Pallas kernels, pack(): pl.pallas_call(functools.partial(pack_kernel, levels, blocks), in_specs=[...  4.63 us
    pallas_call x1, Pallas kernels, merge_most(): pl.pallas_call(functools.partial(most_kernel, levels), in_specs=[SCALARS]...  3.51 us
    pallas_call x1, Pallas kernels, merge_last(): pl.pallas_call(functools.partial(last_kernel, levels), in_specs=[SCALARS]...  2.6 us
  transfers between devices with their start and end apart: 4, of which 4 were waited for; matrix products, arithmetic and copies ran while one was open for 0% of the time, Pallas kernels for 26%

profile of v1, /device:TPU:26, one launch (start us, length us, event | category | flops | bytes accessed | tf_op | source)
XLA Modules:
  0.0 97.4 jit_solution(2034777658956957879)
XLA Ops:
  0.6 0.0 copy-start.3
  0.6 0.0 copy-start.2
  0.7 0.0 copy-start.1
  0.7 0.0 copy-start
  0.7 0.0 copy-start.5
  0.7 4.6 %pack.1 = (s32[16]{0:T(128)}, s32[1]{0:T(128)}, s32[1]{0:T(128)}, bf16[896,512]{1,0:T(8,128)(2,1)}, bf16[896,512]{1,0:T(8,128)(2,1)}) custom-call(s32[32]{0:T(128)} %lengths.3, bf16[512,768]{1,0:T(8,128)(2,1)} %query.5, bf16[512,768]{1,0:T(8,128)(2,1)} %key.5, bf16[512,768]{1,0:T(8,128)(2,1)} %value.5, bf16[512,768]{1,0:T(8,128)(2,1)} %grad.5), custom_call_target="tpu_custom_call" | custom-call | tf_op jit(solution)/shard_map/pack/pallas_call | solution.py:311
  5.3 3.4 %collective-permute-start = (bf16[896,512]{1,0:T(8,128)(2,1)}, bf16[896,512]{1,0:T(8,128)(2,1)S(1)}, u32[]{:S(2)}, u32[]{:S(2)}) collective-permute-start(bf16[896,512]{1,0:T(8,128)(2,1)} %get-tuple-element.27), channel_id=1, source_target_pairs={{4,8},{12,16},{20,24},{8,4},{16,12},{24,20},{5,9},{13,17},{21,25},... | collective-permute-start | bytes 2752520 | tf_op jit(solution)/shard_map/ppermute | solution.py:598
  8.7 0.0 copy-start.4
  8.7 0.1 collective-permute-start.1
  8.8 0.0 copy-done.3
  8.8 0.0 copy-done.2
  8.8 0.0 copy-done.1
  8.8 0.0 copy-done
  8.8 0.0 copy-done.5
  8.8 9.6 %local_images.1 = (bf16[512,768]{1,0:T(8,128)(2,1)S(1)}, bf16[512,768]{1,0:T(8,128)(2,1)S(1)}, bf16[512,768]{1,0:T(8,128)(2,1)S(1)}, bf16[512,768]{1,0:T(8,128)(2,1)S(1)}) custom-call(s32[32]{0:T(128)S(1)} %copy-done.5, bf16[512,768]{1,0:T(8,128)(2,1)S(1)} %copy-done, bf16[512,768]{1,0:T(8,128)(2,1)S(1)} %copy-done.1, bf16[512,768]{1,0:T(8,128)(2,1)S(1)} %copy-done.2, ...), custom_call_target="tpu_custom_call" | custom-call | flops 2415919104 | bytes 6291456 | tf_op jit(solution)/shard_map/local_images/pallas_call | solution.py:221
  18.4 12.1 %collective-permute-done.rest_0_ = bf16[896,512]{1,0:T(8,128)(2,1)S(1)} collective-permute-done((bf16[896,512]{1,0:T(8,128)(2,1)}, bf16[896,512]{1,0:T(8,128)(2,1)S(1)}, u32[]{:S(2)}, u32[]{:S(2)}) %collective-permute-start) | collective-permute-done | bytes 917536 | tf_op jit(solution)/shard_map/ppermute | solution.py:598
  30.5 0.0 copy-done.4
  30.5 6.0 %even_edge_images.1 = (bf16[896,512]{1,0:T(8,128)(2,1)S(1)}, bf16[6,512,512]{2,1,0:T(8,128)(2,1)S(1)}) custom-call(s32[16]{0:T(128)S(1)} %copy-done.4, bf16[512,768]{1,0:T(8,128)(2,1)S(1)} %copy-done, bf16[512,768]{1,0:T(8,128)(2,1)S(1)} %copy-done.1, bf16[512,768]{1,0:T(8,128)(2,1)S(1)} %copy-done.2, bf16[512,768]{1,0:T(8,128)(2,1)S(1)} %copy-done.3, ...), custom_call_target="tpu_custom_call" | custom-call | tf_op jit(solution)/shard_map/even_edge_images/pallas_call | solution.py:414
  36.5 13.6 %collective-permute-done.1.rest_0_ = bf16[896,512]{1,0:T(8,128)(2,1)S(1)} collective-permute-done((bf16[896,512]{1,0:T(8,128)(2,1)}, bf16[896,512]{1,0:T(8,128)(2,1)S(1)}, u32[]{:S(2)}, u32[]{:S(2)}) %collective-permute-start.1) | collective-permute-done | bytes 917536 | tf_op jit(solution)/shard_map/ppermute | solution.py:598
  50.1 3.4 %collective-permute-start.3 = (bf16[896,512]{1,0:T(8,128)(2,1)S(1)}, bf16[896,512]{1,0:T(8,128)(2,1)S(1)}, u32[]{:S(2)}, u32[]{:S(2)}) collective-permute-start(bf16[896,512]{1,0:T(8,128)(2,1)S(1)} %get-tuple-element.39), channel_id=1, source_target_pairs={{4,8},{12,16},{20,24},{8,4},{16,12},{24,20},{5,9},{13,17},{21,25},... | collective-permute-start | bytes 2752520 | tf_op jit(solution)/shard_map/ppermute | solution.py:598
  53.4 6.1 %odd_edge_images.1 = (bf16[896,512]{1,0:T(8,128)(2,1)S(1)}, bf16[6,512,512]{2,1,0:T(8,128)(2,1)S(1)}) custom-call(s32[16]{0:T(128)S(1)} %copy-done.4, bf16[512,768]{1,0:T(8,128)(2,1)S(1)} %copy-done, bf16[512,768]{1,0:T(8,128)(2,1)S(1)} %copy-done.1, bf16[512,768]{1,0:T(8,128)(2,1)S(1)} %copy-done.2, bf16[512,768]{1,0:T(8,128)(2,1)S(1)} %copy-done.3, ...), custom_call_target="tpu_custom_call" | custom-call | tf_op jit(solution)/shard_map/odd_edge_images/pallas_call | solution.py:414
  59.6 0.1 collective-permute-start.2
  59.6 15.6 %collective-permute-done.3.rest_0_ = bf16[896,512]{1,0:T(8,128)(2,1)S(1)} collective-permute-done((bf16[896,512]{1,0:T(8,128)(2,1)S(1)}, bf16[896,512]{1,0:T(8,128)(2,1)S(1)}, u32[]{:S(2)}, u32[]{:S(2)}) %collective-permute-start.3) | collective-permute-done | bytes 917536 | tf_op jit(solution)/shard_map/ppermute | solution.py:598
  75.2 3.5 %merge_most.1 = (bf16[512,768]{1,0:T(8,128)(2,1)}, bf16[512,768]{1,0:T(8,128)(2,1)}, bf16[512,768]{1,0:T(8,128)(2,1)}, bf16[512,768]{1,0:T(8,128)(2,1)}) custom-call(s32[16]{0:T(128)S(1)} %copy-done.4, bf16[6,512,512]{2,1,0:T(8,128)(2,1)S(1)} %get-tuple-element.37.kept_odd, bf16[6,512,512]{2,1,0:T(8,128)(2,1)S(1)} %get-tuple-element.38.kept_even, ...), custom_call_target="tpu_custom_call" | custom-call | bytes 12582912 | tf_op jit(solution)/shard_map/merge_most/pallas_call | solution.py:519
  78.7 16.0 %collective-permute-done.2.rest_0_ = bf16[896,512]{1,0:T(8,128)(2,1)S(1)} collective-permute-done((bf16[896,512]{1,0:T(8,128)(2,1)S(1)}, bf16[896,512]{1,0:T(8,128)(2,1)S(1)}, u32[]{:S(2)}, u32[]{:S(2)}) %collective-permute-start.2) | collective-permute-done | bytes 917536 | tf_op jit(solution)/shard_map/ppermute | solution.py:598
  94.8 2.6 %merge_last.1 = (bf16[512,768]{1,0:T(8,128)(2,1)}, bf16[512,768]{1,0:T(8,128)(2,1)}, bf16[512,768]{1,0:T(8,128)(2,1)}, bf16[512,768]{1,0:T(8,128)(2,1)}) custom-call(s32[16]{0:T(128)S(1)} %copy-done.4, bf16[896,512]{1,0:T(8,128)(2,1)S(1)} %collective-permute-done.2.rest_0_, ...), custom_call_target="tpu_custom_call", output_to_operand_aliasing={{0}: (2, {}), {1}: (3, {}), {2}: (4, {}), {3}: (5, {})} | custom-call | tf_op jit(solution)/shard_map/merge_last/pallas_call | solution.py:578
Async XLA Ops:
  0.6 8.2 %copy-start.3 = (bf16[512,768]{1,0:T(8,128)(2,1)S(1)}, bf16[512,768]{1,0:T(8,128)(2,1)}, u32[]{:S(2)}) copy-start(bf16[512,768]{1,0:T(8,128)(2,1)} %grad.5) | copy-start | bytes 2359300
  0.6 8.2 %copy-start.2 = (bf16[512,768]{1,0:T(8,128)(2,1)S(1)}, bf16[512,768]{1,0:T(8,128)(2,1)}, u32[]{:S(2)}) copy-start(bf16[512,768]{1,0:T(8,128)(2,1)} %value.5) | copy-start | bytes 2359300
  0.7 8.2 %copy-start.1 = (bf16[512,768]{1,0:T(8,128)(2,1)S(1)}, bf16[512,768]{1,0:T(8,128)(2,1)}, u32[]{:S(2)}) copy-start(bf16[512,768]{1,0:T(8,128)(2,1)} %key.5) | copy-start | bytes 2359300
  0.7 8.2 %copy-start = (bf16[512,768]{1,0:T(8,128)(2,1)S(1)}, bf16[512,768]{1,0:T(8,128)(2,1)}, u32[]{:S(2)}) copy-start(bf16[512,768]{1,0:T(8,128)(2,1)} %query.5) | copy-start | bytes 2359300
  0.7 8.2 %copy-start.5 = (s32[32]{0:T(128)S(1)}, s32[32]{0:T(128)}, u32[]{:S(2)}) copy-start(s32[32]{0:T(128)} %lengths.3) | copy-start | bytes 388
  5.3 25.2 %collective-permute-start = (bf16[896,512]{1,0:T(8,128)(2,1)}, bf16[896,512]{1,0:T(8,128)(2,1)S(1)}, u32[]{:S(2)}, u32[]{:S(2)}) collective-permute-start(bf16[896,512]{1,0:T(8,128)(2,1)} %get-tuple-element.27), channel_id=1, source_target_pairs={{4,8},{12,16},{20,24},{8,4},{16,12},{24,20},{5,9},{13,17},{21,25},... | collective-permute-start | bytes 2752520 | tf_op jit(solution)/shard_map/ppermute | solution.py:598
  8.7 21.8 %copy-start.4 = (s32[16]{0:T(128)S(1)}, s32[16]{0:T(128)}, u32[]{:S(2)}) copy-start(s32[16]{0:T(128)} %get-tuple-element.26.plan) | copy-start | bytes 196
  8.7 41.4 %collective-permute-start.1 = (bf16[896,512]{1,0:T(8,128)(2,1)}, bf16[896,512]{1,0:T(8,128)(2,1)S(1)}, u32[]{:S(2)}, u32[]{:S(2)}) collective-permute-start(bf16[896,512]{1,0:T(8,128)(2,1)} %get-tuple-element.34), channel_id=1, source_target_pairs={{0,4},{8,12},{16,20},{24,28},{4,0},{12,8},{20,16},{28,24},{1,5},{9... | collective-permute-start | bytes 2752520 | tf_op jit(solution)/shard_map/ppermute | solution.py:598
  50.1 25.2 %collective-permute-start.3 = (bf16[896,512]{1,0:T(8,128)(2,1)S(1)}, bf16[896,512]{1,0:T(8,128)(2,1)S(1)}, u32[]{:S(2)}, u32[]{:S(2)}) collective-permute-start(bf16[896,512]{1,0:T(8,128)(2,1)S(1)} %get-tuple-element.39), channel_id=1, source_target_pairs={{4,8},{12,16},{20,24},{8,4},{16,12},{24,20},{5,9},{13,17},{21,25},... | collective-permute-start | bytes 2752520 | tf_op jit(solution)/shard_map/ppermute | solution.py:598
  59.6 35.2 %collective-permute-start.2 = (bf16[896,512]{1,0:T(8,128)(2,1)S(1)}, bf16[896,512]{1,0:T(8,128)(2,1)S(1)}, u32[]{:S(2)}, u32[]{:S(2)}) collective-permute-start(bf16[896,512]{1,0:T(8,128)(2,1)S(1)} %get-tuple-element.36), channel_id=1, source_target_pairs={{0,4},{8,12},{16,20},{24,28},{4,0},{12,8},{20,16},{28,24},{1,5},{9... | collective-permute-start | bytes 2752520 | tf_op jit(solution)/shard_map/ppermute | solution.py:598

commit v2 on v1

--- a/solution.py
+++ b/solution.py
@@ -22,7 +22,7 @@
 BEFORE, AFTER, LOWER, JOBS, JOB_HEAD, SENT, SENT_HEAD, LEVEL = range(FIELDS)
 ODD, EVEN = 0, 1
 
-LEVEL_UNITS = ((), ())
+LEVEL_UNITS = ((12,), (7, 12))
 
 
 def round_up(value):

time: 98.9 us -> 106 us (1.072); the launches traced: 97.4 us -> 106 us
  waiting for transfers between devices: 57.3 us -> 21.2 us
  local copies, waits for them, and re-layouts: 0.03 us -> 18.3 us
  starting transfers between devices: 6.87 us -> 20.4 us
  Pallas kernels: 32.4 us -> 42.7 us
  between operations: 0.79 us -> 3.33 us
    ppermute x4 -> x8, waiting for transfers between devices: 57.3 us -> 21.2 us  [swapped(): lax.ppermute(value, 'dp', pairs + [(after, before) for before, after in p...]
    unnamed x12 -> x44, local copies, waits for them, and re-layouts: 0.03 us -> 17 us
    ppermute x4 -> x8, starting transfers between devices: 6.87 us -> 20.4 us  [swapped(): lax.ppermute(value, 'dp', pairs + [(after, before) for before, after in p...]
    pallas_call x2, Pallas kernels: 12.1 us -> 17.7 us  [crossing_images(): pl.pallas_call(functools.partial(crossing_kernel, levels, kind), in_specs...]
    pallas_call x1, Pallas kernels: 3.51 us -> 7.5 us  [merge_most(): pl.pallas_call(functools.partial(most_kernel, levels), in_specs=[SCALARS]...]
    another operation x0 -> x2, local copies, waits for them, and re-layouts: none -> 1.34 us
  transfers between devices with their start and end apart: 4 -> 8, of which waited for: 4 -> 2; matrix products, arithmetic and copies ran while one was open for 0% -> 1% of each run, Pallas kernels for 26% -> 25%
where the time goes in v2:
time: 106 us
  Pallas kernels  42.7 us (40%)
  waiting for transfers between devices  21.2 us (20%)
  starting transfers between devices  20.4 us (19%)
  local copies, waits for them, and re-layouts  18.3 us (17%)
  between operations  3.33 us (3%)
    ppermute x8, waiting for transfers between devices, swapped(): lax.ppermute(value, 'dp', pairs + [(after, before) for before, after in p...  21.2 us
    ppermute x8, starting transfers between devices, swapped(): lax.ppermute(value, 'dp', pairs + [(after, before) for before, after in p...  20.4 us
    pallas_call x2, Pallas kernels, crossing_images(): pl.pallas_call(functools.partial(crossing_kernel, levels, kind), in_specs...  17.7 us
    unnamed x44, local copies, waits for them, and re-layouts  17 us
    pallas_call x1, Pallas kernels, local_attention(): pl.pallas_call(local_kernel, grid=(heads,), in_specs=[pl.BlockSpec(memory...  9.59 us
    pallas_call x1, Pallas kernels, merge_most(): pl.pallas_call(functools.partial(most_kernel, levels), in_specs=[SCALARS]...  7.5 us
    pallas_call x1, Pallas kernels, pack(): pl.pallas_call(functools.partial(pack_kernel, levels, blocks), in_specs=[...  4.96 us
    pallas_call x1, Pallas kernels, merge_last(): pl.pallas_call(functools.partial(last_kernel, levels), in_specs=[SCALARS]...  2.9 us
  transfers between devices with their start and end apart: 8, of which 2 were waited for; matrix products, arithmetic and copies ran while one was open for 1% of the time, Pallas kernels for 25%

profile of v2, /device:TPU:26, one launch (start us, length us, event | category | flops | bytes accessed | tf_op | source)
XLA Modules:
  0.0 106.0 jit_solution(11213783751304648211)
XLA Ops:
  0.7 5.0 %pack.1 = (s32[16]{0:T(128)}, s32[1]{0:T(128)}, s32[1]{0:T(128)}, bf16[768,512]{1,0:T(8,128)(2,1)}, bf16[128,512]{1,0:T(8,128)(2,1)}, /*index=5*/bf16[448,512]{1...) custom-call(s32[32]{0:T(128)} %lengths.3, bf16[512,768]{1,0:T(8,128)(2,1)} %query.5, ...), custom_call_target="tpu_custom_call" | custom-call | tf_op jit(solution)/shard_map/pack/pallas_call | solution.py:311
  5.7 1.3 %collective-permute-start.9 = (bf16[768,512]{1,0:T(8,128)(2,1)}, bf16[768,512]{1,0:T(8,128)(2,1)}, u32[]{:S(2)}, u32[]{:S(2)}) collective-permute-start(bf16[768,512]{1,0:T(8,128)(2,1)} %get-tuple-element.85), channel_id=1, source_target_pairs={{0,4},{8,12},{16,20},{24,28},{4,0},{12,8},{20,16},{28,24},{1,5},{9... | collective-permute-start | bytes 2359304 | tf_op jit(solution)/shard_map/ppermute | solution.py:598
  7.0 2.4 %collective-permute-start.8 = (bf16[448,512]{1,0:T(8,128)(2,1)}, bf16[448,512]{1,0:T(8,128)(2,1)S(1)}, u32[]{:S(2)}, u32[]{:S(2)}) collective-permute-start(bf16[448,512]{1,0:T(8,128)(2,1)} %get-tuple-element.72), channel_id=1, source_target_pairs={{4,8},{12,16},{20,24},{8,4},{16,12},{24,20},{5,9},{13,17},{21,25},... | collective-permute-start | bytes 1376264 | tf_op jit(solution)/shard_map/ppermute | solution.py:598
  9.5 9.6 %local_images.1 = (bf16[512,768]{1,0:T(8,128)(2,1)S(1)}, bf16[512,768]{1,0:T(8,128)(2,1)S(1)}, bf16[512,768]{1,0:T(8,128)(2,1)S(1)}, bf16[512,768]{1,0:T(8,128)(2,1)S(1)}) custom-call(s32[32]{0:T(128)S(1)} %copy-done.19, bf16[512,768]{1,0:T(8,128)(2,1)S(1)} %copy-done, bf16[512,768]{1,0:T(8,128)(2,1)S(1)} %copy-done.1, bf16[512,768]{1,0:T(8,128)(2,1)S(1)} %copy-done.2, ...), custom_call_target="tpu_custom_call" | custom-call | flops 2415919104 | bytes 6291456 | tf_op jit(solution)/shard_map/local_images/pallas_call | solution.py:221
  19.1 0.9 copy-done.8
  20.0 0.9 copy-done.10
  20.9 0.9 copy-done.12
  21.7 0.9 copy-done.14
  22.6 0.8 copy-done.16
  24.0 14.7 %conditional.4 = (bf16[320,512]{1,0:T(8,128)(2,1)}, bf16[128,512]{1,0:T(8,128)(2,1)}) conditional(s32[]{:T(128)} %bitcast, () %tuple.49, bf16[320,512]{1,0:T(8,128)(2,1)S(1)} %get-tuple-element.80, (bf16[320,512]{1,0:T(8,128)(2,1)S(1)}, bf16[128,512]{1,0:T(8,128)(2,1)S(1)}) %tuple.50), branch_computations={%region_0.0_spmd, %region_1.0_spmd, %region_2.0_spmd} | conditional | bytes 1835104 | solution.py:612
  24.1 4.3 %collective-permute-start.1 = (bf16[320,512]{1,0:T(8,128)(2,1)S(1)}, bf16[320,512]{1,0:T(8,128)(2,1)}, u32[]{:S(2)}, u32[]{:S(2)}) collective-permute-start(bf16[320,512]{1,0:T(8,128)(2,1)S(1)} %get-tuple-element.18), channel_id=1, source_target_pairs={{4,8},{12,16},{20,24},{8,4},{16,12},{24,20},{5,9},{13,17},{21,25},... | collective-permute-start | bytes 983048 | tf_op jit(solution)/shard_map/cond/branch_2_fun/ppermute | solution.py:598
  28.4 2.4 %collective-permute-start.2 = (bf16[128,512]{1,0:T(8,128)(2,1)S(1)}, bf16[128,512]{1,0:T(8,128)(2,1)}, u32[]{:S(2)}, u32[]{:S(2)}) collective-permute-start(bf16[128,512]{1,0:T(8,128)(2,1)S(1)} %get-tuple-element.19), channel_id=1, source_target_pairs={{4,8},{12,16},{20,24},{8,4},{16,12},{24,20},{5,9},{13,17},{21,25},... | collective-permute-start | bytes 393224 | tf_op jit(solution)/shard_map/cond/branch_2_fun/ppermute | solution.py:598
  30.8 8.0 %collective-permute-done.2 = bf16[128,512]{1,0:T(8,128)(2,1)} collective-permute-done((bf16[128,512]{1,0:T(8,128)(2,1)S(1)}, bf16[128,512]{1,0:T(8,128)(2,1)}, u32[]{:S(2)}, u32[]{:S(2)}) %collective-permute-start.2) | collective-permute-done | bytes 131104 | tf_op jit(solution)/shard_map/cond/branch_2_fun/ppermute | solution.py:598
  38.8 1.0 copy-done.17
  39.8 9.5 %even_edge_images.1 = (bf16[448,512]{1,0:T(8,128)(2,1)}, bf16[320,512]{1,0:T(8,128)(2,1)S(1)}, bf16[128,512]{1,0:T(8,128)(2,1)}, bf16[6,512,512]{2,1,0:T(8,128)(2,1)S(1)}) custom-call(s32[16]{0:T(128)S(1)} %copy-done.18, bf16[512,768]{1,0:T(8,128)(2,1)S(1)} %copy-done, bf16[512,768]{1,0:T(8,128)(2,1)S(1)} %copy-done.1, bf16[512,768]{1,0:T(8,128)(2,1)S(1)} %copy-done.2, ...), custom_call_target="tpu_custom_call" | custom-call | tf_op jit(solution)/shard_map/even_edge_images/pallas_call | solution.py:414
  49.4 1.6 %copy-done.4 = bf16[6,512,512]{2,1,0:T(8,128)(2,1)} copy-done((bf16[6,512,512]{2,1,0:T(8,128)(2,1)}, bf16[6,512,512]{2,1,0:T(8,128)(2,1)S(1)}, u32[]{:S(2)}) %copy-start.4) | copy-done | bytes 3145752
  51.6 0.7 conditional.5
  52.3 8.2 %odd_edge_images.1 = (bf16[768,512]{1,0:T(8,128)(2,1)}, bf16[128,512]{1,0:T(8,128)(2,1)}, bf16[6,512,512]{2,1,0:T(8,128)(2,1)S(1)}) custom-call(s32[16]{0:T(128)S(1)} %copy-done.18, bf16[512,768]{1,0:T(8,128)(2,1)S(1)} %copy-done, bf16[512,768]{1,0:T(8,128)(2,1)S(1)} %copy-done.1, bf16[512,768]{1,0:T(8,128)(2,1)S(1)} %copy-done.2, ...), custom_call_target="tpu_custom_call" | custom-call | tf_op jit(solution)/shard_map/odd_edge_images/pallas_call | solution.py:414
  60.5 1.7 %copy-done.6 = bf16[6,512,512]{2,1,0:T(8,128)(2,1)} copy-done((bf16[6,512,512]{2,1,0:T(8,128)(2,1)}, bf16[6,512,512]{2,1,0:T(8,128)(2,1)S(1)}, u32[]{:S(2)}) %copy-start.6) | copy-done | bytes 3145752
  62.2 3.1 %collective-permute-start.11 = (bf16[448,512]{1,0:T(8,128)(2,1)}, bf16[448,512]{1,0:T(8,128)(2,1)S(1)}, u32[]{:S(2)}, u32[]{:S(2)}) collective-permute-start(bf16[448,512]{1,0:T(8,128)(2,1)} %get-tuple-element.96), channel_id=1, source_target_pairs={{4,8},{12,16},{20,24},{8,4},{16,12},{24,20},{5,9},{13,17},{21,25},... | collective-permute-start | bytes 1376264 | tf_op jit(solution)/shard_map/ppermute | solution.py:598
  66.0 20.0 %conditional.6 = (bf16[320,512]{1,0:T(8,128)(2,1)}, bf16[128,512]{1,0:T(8,128)(2,1)}) conditional(s32[]{:T(128)} %bitcast.2, () %tuple.55, bf16[320,512]{1,0:T(8,128)(2,1)S(1)} %get-tuple-element.98, (bf16[320,512]{1,0:T(8,128)(2,1)S(1)}, bf16[128,512]{1,0:T(8,128)(2,1)S(1)}) %tuple.69), branch_computations={%region_5.0_spmd, %region_6.0_spmd, %region_7.0_spmd} | conditional | bytes 1835104 | solution.py:612
  66.0 3.6 %collective-permute-start.5 = (bf16[320,512]{1,0:T(8,128)(2,1)S(1)}, bf16[320,512]{1,0:T(8,128)(2,1)}, u32[]{:S(2)}, u32[]{:S(2)}) collective-permute-start(bf16[320,512]{1,0:T(8,128)(2,1)S(1)} %get-tuple-element.20), channel_id=1, source_target_pairs={{4,8},{12,16},{20,24},{8,4},{16,12},{24,20},{5,9},{13,17},{21,25},... | collective-permute-start | bytes 983048 | tf_op jit(solution)/shard_map/cond/branch_2_fun/ppermute | solution.py:598
  69.6 3.2 %collective-permute-start.6 = (bf16[128,512]{1,0:T(8,128)(2,1)S(1)}, bf16[128,512]{1,0:T(8,128)(2,1)}, u32[]{:S(2)}, u32[]{:S(2)}) collective-permute-start(bf16[128,512]{1,0:T(8,128)(2,1)S(1)} %get-tuple-element.21), channel_id=1, source_target_pairs={{4,8},{12,16},{20,24},{8,4},{16,12},{24,20},{5,9},{13,17},{21,25},... | collective-permute-start | bytes 393224 | tf_op jit(solution)/shard_map/cond/branch_2_fun/ppermute | solution.py:598
  72.8 13.2 %collective-permute-done.6 = bf16[128,512]{1,0:T(8,128)(2,1)} collective-permute-done((bf16[128,512]{1,0:T(8,128)(2,1)S(1)}, bf16[128,512]{1,0:T(8,128)(2,1)}, u32[]{:S(2)}, u32[]{:S(2)}) %collective-permute-start.6) | collective-permute-done | bytes 131104 | tf_op jit(solution)/shard_map/cond/branch_2_fun/ppermute | solution.py:598
  86.0 1.9 %copy-done.5 = bf16[6,512,512]{2,1,0:T(8,128)(2,1)S(1)} copy-done((bf16[6,512,512]{2,1,0:T(8,128)(2,1)S(1)}, bf16[6,512,512]{2,1,0:T(8,128)(2,1)}, u32[]{:S(2)}) %copy-start.5) | copy-done | bytes 3145752
  87.9 1.9 %copy-done.7 = bf16[6,512,512]{2,1,0:T(8,128)(2,1)S(1)} copy-done((bf16[6,512,512]{2,1,0:T(8,128)(2,1)S(1)}, bf16[6,512,512]{2,1,0:T(8,128)(2,1)}, u32[]{:S(2)}) %copy-start.7) | copy-done | bytes 3145752
  89.8 1.1 %copy-done.9 = bf16[512,768]{1,0:T(8,128)(2,1)S(1)} copy-done((bf16[512,768]{1,0:T(8,128)(2,1)S(1)}, bf16[512,768]{1,0:T(8,128)(2,1)}, u32[]{:S(2)}) %copy-start.9) | copy-done | bytes 786456
  90.9 1.1 %copy-done.11 = bf16[512,768]{1,0:T(8,128)(2,1)S(1)} copy-done((bf16[512,768]{1,0:T(8,128)(2,1)S(1)}, bf16[512,768]{1,0:T(8,128)(2,1)}, u32[]{:S(2)}) %copy-start.11) | copy-done | bytes 786456
  92.1 1.1 %copy-done.13 = bf16[512,768]{1,0:T(8,128)(2,1)S(1)} copy-done((bf16[512,768]{1,0:T(8,128)(2,1)S(1)}, bf16[512,768]{1,0:T(8,128)(2,1)}, u32[]{:S(2)}) %copy-start.13) | copy-done | bytes 786456
  93.2 1.1 %copy-done.15 = bf16[512,768]{1,0:T(8,128)(2,1)S(1)} copy-done((bf16[512,768]{1,0:T(8,128)(2,1)S(1)}, bf16[512,768]{1,0:T(8,128)(2,1)}, u32[]{:S(2)}) %copy-start.15) | copy-done | bytes 786456
  94.3 7.5 %merge_most.1 = (bf16[512,768]{1,0:T(8,128)(2,1)}, bf16[512,768]{1,0:T(8,128)(2,1)}, bf16[512,768]{1,0:T(8,128)(2,1)}, bf16[512,768]{1,0:T(8,128)(2,1)}) custom-call(s32[16]{0:T(128)S(1)} %copy-done.18, bf16[6,512,512]{2,1,0:T(8,128)(2,1)S(1)} %copy-done.7, bf16[6,512,512]{2,1,0:T(8,128)(2,1)S(1)} %copy-done.5, ...), custom_call_target="tpu_custom_call" | custom-call | bytes 12582912 | tf_op jit(solution)/shard_map/merge_most/pallas_call | solution.py:519
  103.1 2.9 %merge_last.1 = (bf16[512,768]{1,0:T(8,128)(2,1)}, bf16[512,768]{1,0:T(8,128)(2,1)}, bf16[512,768]{1,0:T(8,128)(2,1)}, bf16[512,768]{1,0:T(8,128)(2,1)}) custom-call(s32[16]{0:T(128)S(1)} %copy-done.18, bf16[768,512]{1,0:T(8,128)(2,1)S(1)} %collective-permute-done.10.rest_0_, ...), custom_call_target="tpu_custom_call", output_to_operand_aliasing={{0}: (3, {}), {1}: (4, {}), {2}: (5, {}), {3}: (6, {})} | custom-call | tf_op jit(solution)/shard_map/merge_last/pallas_call | solution.py:578
  (40 shorter events, 2.1 us)
Async XLA Ops:
  0.6 8.8 %copy-start.3 = (bf16[512,768]{1,0:T(8,128)(2,1)S(1)}, bf16[512,768]{1,0:T(8,128)(2,1)}, u32[]{:S(2)}) copy-start(bf16[512,768]{1,0:T(8,128)(2,1)} %grad.5) | copy-start | bytes 2359300
  0.6 8.8 %copy-start.2 = (bf16[512,768]{1,0:T(8,128)(2,1)S(1)}, bf16[512,768]{1,0:T(8,128)(2,1)}, u32[]{:S(2)}) copy-start(bf16[512,768]{1,0:T(8,128)(2,1)} %value.5) | copy-start | bytes 2359300
  0.7 8.8 %copy-start.1 = (bf16[512,768]{1,0:T(8,128)(2,1)S(1)}, bf16[512,768]{1,0:T(8,128)(2,1)}, u32[]{:S(2)}) copy-start(bf16[512,768]{1,0:T(8,128)(2,1)} %key.5) | copy-start | bytes 2359300
  0.7 8.8 %copy-start = (bf16[512,768]{1,0:T(8,128)(2,1)S(1)}, bf16[512,768]{1,0:T(8,128)(2,1)}, u32[]{:S(2)}) copy-start(bf16[512,768]{1,0:T(8,128)(2,1)} %query.5) | copy-start | bytes 2359300
  0.7 8.8 %copy-start.19 = (s32[32]{0:T(128)S(1)}, s32[32]{0:T(128)}, u32[]{:S(2)}) copy-start(s32[32]{0:T(128)} %lengths.3) | copy-start | bytes 388
  5.7 46.7 %collective-permute-start.9 = (bf16[768,512]{1,0:T(8,128)(2,1)}, bf16[768,512]{1,0:T(8,128)(2,1)}, u32[]{:S(2)}, u32[]{:S(2)}) collective-permute-start(bf16[768,512]{1,0:T(8,128)(2,1)} %get-tuple-element.85), channel_id=1, source_target_pairs={{0,4},{8,12},{16,20},{24,28},{4,0},{12,8},{20,16},{28,24},{1,5},{9... | collective-permute-start | bytes 2359304 | tf_op jit(solution)/shard_map/ppermute | solution.py:598
  7.0 15.6 %collective-permute-start.8 = (bf16[448,512]{1,0:T(8,128)(2,1)}, bf16[448,512]{1,0:T(8,128)(2,1)S(1)}, u32[]{:S(2)}, u32[]{:S(2)}) collective-permute-start(bf16[448,512]{1,0:T(8,128)(2,1)} %get-tuple-element.72), channel_id=1, source_target_pairs={{4,8},{12,16},{20,24},{8,4},{16,12},{24,20},{5,9},{13,17},{21,25},... | collective-permute-start | bytes 1376264 | tf_op jit(solution)/shard_map/ppermute | solution.py:598
  9.5 29.3 %copy-start.18 = (s32[16]{0:T(128)S(1)}, s32[16]{0:T(128)}, u32[]{:S(2)}) copy-start(s32[16]{0:T(128)} %get-tuple-element.71.plan) | copy-start | bytes 196
  19.1 0.9 copy-start.8
  20.0 0.9 copy-start.10
  20.9 0.9 copy-start.12
  21.7 0.9 copy-start.14
  22.6 0.8 copy-start.16
  24.1 14.7 %collective-permute-start.1 = (bf16[320,512]{1,0:T(8,128)(2,1)S(1)}, bf16[320,512]{1,0:T(8,128)(2,1)}, u32[]{:S(2)}, u32[]{:S(2)}) collective-permute-start(bf16[320,512]{1,0:T(8,128)(2,1)S(1)} %get-tuple-element.18), channel_id=1, source_target_pairs={{4,8},{12,16},{20,24},{8,4},{16,12},{24,20},{5,9},{13,17},{21,25},... | collective-permute-start | bytes 983048 | tf_op jit(solution)/shard_map/cond/branch_2_fun/ppermute | solution.py:598
  28.4 10.4 %collective-permute-start.2 = (bf16[128,512]{1,0:T(8,128)(2,1)S(1)}, bf16[128,512]{1,0:T(8,128)(2,1)}, u32[]{:S(2)}, u32[]{:S(2)}) collective-permute-start(bf16[128,512]{1,0:T(8,128)(2,1)S(1)} %get-tuple-element.19), channel_id=1, source_target_pairs={{4,8},{12,16},{20,24},{8,4},{16,12},{24,20},{5,9},{13,17},{21,25},... | collective-permute-start | bytes 393224 | tf_op jit(solution)/shard_map/cond/branch_2_fun/ppermute | solution.py:598
  38.8 1.0 copy-start.17
  49.3 1.6 %copy-start.4 = (bf16[6,512,512]{2,1,0:T(8,128)(2,1)}, bf16[6,512,512]{2,1,0:T(8,128)(2,1)S(1)}, u32[]{:S(2)}) copy-start(bf16[6,512,512]{2,1,0:T(8,128)(2,1)S(1)} %get-tuple-element.95.kept_even) | copy-start | bytes 9437188
  52.3 13.7 %copy-start.21 = (bf16[128,512]{1,0:T(8,128)(2,1)S(1)}, bf16[128,512]{1,0:T(8,128)(2,1)}, u32[]{:S(2)}) copy-start(bf16[128,512]{1,0:T(8,128)(2,1)} %get-tuple-element.99) | copy-start | bytes 393220
  60.5 1.7 %copy-start.6 = (bf16[6,512,512]{2,1,0:T(8,128)(2,1)}, bf16[6,512,512]{2,1,0:T(8,128)(2,1)S(1)}, u32[]{:S(2)}) copy-start(bf16[6,512,512]{2,1,0:T(8,128)(2,1)S(1)} %get-tuple-element.94.kept_odd) | copy-start | bytes 9437188
  62.2 40.9 %collective-permute-start.10 = (bf16[768,512]{1,0:T(8,128)(2,1)}, bf16[768,512]{1,0:T(8,128)(2,1)S(1)}, u32[]{:S(2)}, u32[]{:S(2)}) collective-permute-start(bf16[768,512]{1,0:T(8,128)(2,1)} %get-tuple-element.92), channel_id=1, source_target_pairs={{0,4},{8,12},{16,20},{24,28},{4,0},{12,8},{20,16},{28,24},{1,5},{9... | collective-permute-start | bytes 2359304 | tf_op jit(solution)/shard_map/ppermute | solution.py:598
  62.2 23.8 %collective-permute-start.11 = (bf16[448,512]{1,0:T(8,128)(2,1)}, bf16[448,512]{1,0:T(8,128)(2,1)S(1)}, u32[]{:S(2)}, u32[]{:S(2)}) collective-permute-start(bf16[448,512]{1,0:T(8,128)(2,1)} %get-tuple-element.96), channel_id=1, source_target_pairs={{4,8},{12,16},{20,24},{8,4},{16,12},{24,20},{5,9},{13,17},{21,25},... | collective-permute-start | bytes 1376264 | tf_op jit(solution)/shard_map/ppermute | solution.py:598
  66.0 20.0 %collective-permute-start.5 = (bf16[320,512]{1,0:T(8,128)(2,1)S(1)}, bf16[320,512]{1,0:T(8,128)(2,1)}, u32[]{:S(2)}, u32[]{:S(2)}) collective-permute-start(bf16[320,512]{1,0:T(8,128)(2,1)S(1)} %get-tuple-element.20), channel_id=1, source_target_pairs={{4,8},{12,16},{20,24},{8,4},{16,12},{24,20},{5,9},{13,17},{21,25},... | collective-permute-start | bytes 983048 | tf_op jit(solution)/shard_map/cond/branch_2_fun/ppermute | solution.py:598
  69.6 16.4 %collective-permute-start.6 = (bf16[128,512]{1,0:T(8,128)(2,1)S(1)}, bf16[128,512]{1,0:T(8,128)(2,1)}, u32[]{:S(2)}, u32[]{:S(2)}) collective-permute-start(bf16[128,512]{1,0:T(8,128)(2,1)S(1)} %get-tuple-element.21), channel_id=1, source_target_pairs={{4,8},{12,16},{20,24},{8,4},{16,12},{24,20},{5,9},{13,17},{21,25},... | collective-permute-start | bytes 393224 | tf_op jit(solution)/shard_map/cond/branch_2_fun/ppermute | solution.py:598
  86.0 1.9 %copy-start.5 = (bf16[6,512,512]{2,1,0:T(8,128)(2,1)S(1)}, bf16[6,512,512]{2,1,0:T(8,128)(2,1)}, u32[]{:S(2)}) copy-start(bf16[6,512,512]{2,1,0:T(8,128)(2,1)} %copy-done.4) | copy-start | bytes 9437188
  87.9 1.9 %copy-start.7 = (bf16[6,512,512]{2,1,0:T(8,128)(2,1)S(1)}, bf16[6,512,512]{2,1,0:T(8,128)(2,1)}, u32[]{:S(2)}) copy-start(bf16[6,512,512]{2,1,0:T(8,128)(2,1)} %copy-done.6) | copy-start | bytes 9437188
  89.8 1.1 %copy-start.9 = (bf16[512,768]{1,0:T(8,128)(2,1)S(1)}, bf16[512,768]{1,0:T(8,128)(2,1)}, u32[]{:S(2)}) copy-start(bf16[512,768]{1,0:T(8,128)(2,1)} %copy-done.8) | copy-start | bytes 2359300
  90.9 1.1 %copy-start.11 = (bf16[512,768]{1,0:T(8,128)(2,1)S(1)}, bf16[512,768]{1,0:T(8,128)(2,1)}, u32[]{:S(2)}) copy-start(bf16[512,768]{1,0:T(8,128)(2,1)} %copy-done.10) | copy-start | bytes 2359300
  92.1 1.1 %copy-start.13 = (bf16[512,768]{1,0:T(8,128)(2,1)S(1)}, bf16[512,768]{1,0:T(8,128)(2,1)}, u32[]{:S(2)}) copy-start(bf16[512,768]{1,0:T(8,128)(2,1)} %copy-done.12) | copy-start | bytes 2359300
  93.2 1.1 %copy-start.15 = (bf16[512,768]{1,0:T(8,128)(2,1)S(1)}, bf16[512,768]{1,0:T(8,128)(2,1)}, u32[]{:S(2)}) copy-start(bf16[512,768]{1,0:T(8,128)(2,1)} %copy-done.14) | copy-start | bytes 2359300
  94.3 8.1 %copy-start.20 = (bf16[128,512]{1,0:T(8,128)(2,1)S(1)}, bf16[128,512]{1,0:T(8,128)(2,1)}, u32[]{:S(2)}) copy-start(bf16[128,512]{1,0:T(8,128)(2,1)} %get-tuple-element.111) | copy-start | bytes 393220

commit v3 on v2

--- a/solution.py
+++ b/solution.py
@@ -22,7 +22,7 @@
 BEFORE, AFTER, LOWER, JOBS, JOB_HEAD, SENT, SENT_HEAD, LEVEL = range(FIELDS)
 ODD, EVEN = 0, 1
 
-LEVEL_UNITS = ((12,), (7, 12))
+LEVEL_UNITS = ((9, 12), (9, 12))
 
 
 def round_up(value):
@@ -223,14 +223,14 @@
         grid=(heads,),
         in_specs=[pl.BlockSpec(memory_space=pltpu.SMEM)] + [block] * 4,
         out_specs=[block] * 4,
-        out_shape=[jax.ShapeDtypeStruct((rows, width), jnp.bfloat16)] * 4,
+        out_shape=[pltpu.HBM((rows, width), jnp.bfloat16)] * 4,
         scratch_shapes=[pltpu.VMEM((8, rows), jnp.float32)],
         compiler_params=pltpu.CompilerParams(vmem_limit_bytes=VMEM_LIMIT),
         cost_estimate=pl.CostEstimate(
             flops=12 * rows * rows * width, bytes_accessed=16 * rows * width, transcendentals=0
         ),
         name="local_images",
-    )(lengths, *arrays)
+    )(lengths, *in_hbm(arrays))
 
 
 START = lambda copy: copy.start()
@@ -239,13 +239,16 @@
 SCALARS = pl.BlockSpec(memory_space=pltpu.SMEM)
 
 
+def in_hbm(arrays):
+    return [pltpu.with_memory_space_constraint(array, pltpu.HBM) for array in arrays]
+
+
 def pieces(levels):
-    starts = (0,) + levels[:-1]
-    return [(start, end - start) for start, end in zip(starts, levels)]
+    return [(0, levels[0])] + [(levels[0], level - levels[0]) for level in levels[1:]]
 
 
 def piece_shapes(levels):
-    return [jax.ShapeDtypeStruct((size, 4 * HEAD_DIM), jnp.bfloat16) for _, size in pieces(levels)]
+    return [pltpu.HBM((size, 4 * HEAD_DIM), jnp.bfloat16) for _, size in pieces(levels)]
 
 
 def copy_pieces(levels, level, staged, offset, arrays, sems, out, action):
@@ -254,7 +257,7 @@
         outside = arrays[number]
         source, target = (inside, outside) if out else (outside, inside)
 
-        @pl.when(True if number == 0 else level >= number)
+        @pl.when(True if number == 0 else level == number)
         def _():
             action(pltpu.make_async_copy(source, target, sems.at[number]))
 
@@ -326,7 +329,7 @@
         ],
         compiler_params=pltpu.CompilerParams(vmem_limit_bytes=PACK_VMEM_LIMIT),
         name="pack",
-    )(lengths, *arrays)
+    )(lengths, *in_hbm(arrays))
     return plan, (odd_level, even_level), (outs[:counts[0]], outs[counts[0]:])
 
 
@@ -416,7 +419,7 @@
         in_specs=[SCALARS] + [ANYWHERE] * (4 + count),
         out_specs=[ANYWHERE] * (count + 1),
         out_shape=piece_shapes(levels)
-        + [jax.ShapeDtypeStruct((heads, rows, four), jnp.bfloat16)],
+        + [pltpu.HBM((heads, rows, four), jnp.bfloat16)],
         scratch_shapes=[
             pltpu.VMEM((4, rows, width), jnp.bfloat16),
             staged,
@@ -428,8 +431,11 @@
             pltpu.SemaphoreType.DMA((2,)),
         ],
         compiler_params=pltpu.CompilerParams(vmem_limit_bytes=VMEM_LIMIT),
+        cost_estimate=pl.CostEstimate(
+            flops=12 * rows * rows * width, bytes_accessed=16 * rows * width, transcendentals=0
+        ),
         name="odd_edge_images" if kind == ODD else "even_edge_images",
-    )(plan, *arrays, *received)
+    )(plan, *in_hbm(arrays), *received)
     return outs[:count], outs[count]
 
 
@@ -459,10 +465,9 @@
     return source
 
 
-def most_kernel(levels, plan, kept_odd, kept_even, *rest):
-    count = len(levels)
-    returned, local, outs = rest[:count], rest[count:count + 4], rest[count + 4:count + 8]
-    whole, held, staged, whole_sem, held_sem, staged_sem, out_sem = rest[count + 8:]
+def keep_kernel(plan, kept_odd, kept_even, *rest):
+    local, outs = rest[:4], rest[4:8]
+    whole, held, whole_sem, held_sem, out_sem = rest[8:]
     rows, width = local[0].shape
     heads = width // HEAD_DIM
     kept = (kept_odd, kept_even)
@@ -487,14 +492,10 @@
         pltpu.make_async_copy(whole.at[which], outs[which], out_sem.at[which])
         for which in range(4)
     ]
-    stage = functools.partial(
-        copy_pieces, levels, edges[EVEN].level, staged, BLOCK, returned, staged_sem, False)
     parts(START)
-    stage(START)
     for copy in loads:
         copy.start()
     parts(WAIT)
-    stage(WAIT)
     for which in range(4):
         columns = slice(which * HEAD_DIM, (which + 1) * HEAD_DIM)
         loads[which].wait()
@@ -503,93 +504,109 @@
                 whole, which, edges[kind], edges[kind].job_head, edges[kind].jobs,
                 lambda slot, first: held[
                     kind, slot, pl.ds(pl.multiple_of(first, BLOCK), BLOCK), columns])
-        edge = edges[EVEN]
-        overlay(whole, which, edge, edge.sent_head, edge.sent,
-                returned_source(edge, staged, columns))
         saves[which].start()
     for copy in saves:
         copy.wait()
 
 
-def merge_most(plan, kept_odd, kept_even, returned, local, levels):
+def merge_kept(plan, kept_odd, kept_even, local):
     rows, width = local[0].shape
     heads = width // HEAD_DIM
-    four = 4 * HEAD_DIM
-    count = len(levels)
     return pl.pallas_call(
-        functools.partial(most_kernel, levels),
-        in_specs=[SCALARS] + [ANYWHERE] * (6 + count),
+        keep_kernel,
+        in_specs=[SCALARS] + [ANYWHERE] * 6,
         out_specs=[ANYWHERE] * 4,
-        out_shape=[jax.ShapeDtypeStruct((rows, width), jnp.bfloat16)] * 4,
+        out_shape=[pltpu.HBM((rows, width), jnp.bfloat16)] * 4,
         scratch_shapes=[
             pltpu.VMEM((4, rows, width), jnp.bfloat16),
-            pltpu.VMEM((2, heads, rows, four), jnp.bfloat16),
-            pltpu.VMEM((levels[-1] + 2 * BLOCK, four), jnp.bfloat16),
+            pltpu.VMEM((2, heads, rows, 4 * HEAD_DIM), jnp.bfloat16),
             pltpu.SemaphoreType.DMA((4,)),
             pltpu.SemaphoreType.DMA((2, heads)),
-            pltpu.SemaphoreType.DMA((count,)),
             pltpu.SemaphoreType.DMA((4,)),
         ],
         compiler_params=pltpu.CompilerParams(vmem_limit_bytes=VMEM_LIMIT),
         cost_estimate=pl.CostEstimate(
             flops=0, bytes_accessed=32 * rows * width, transcendentals=0
         ),
-        name="merge_most",
-    )(plan, kept_odd, kept_even, *returned, *local)
-
-
-def last_kernel(levels, plan, *rest):
-    count = len(levels)
-    returned, outs = rest[:count], rest[count + 4:count + 8]
-    whole, staged, whole_sem, staged_sem = rest[count + 8:]
+        name="merge_kept",
+    )(plan, *in_hbm([kept_odd, kept_even, *local]))
+
+
+def return_kernel(levels, plan, *rest):
+    counts = [len(levels[ODD]), len(levels[EVEN])]
+    total = sum(counts)
+    returned = rest[:counts[ODD]], rest[counts[ODD]:total]
+    outs = rest[total + 4:total + 8]
+    whole, odd_staged, even_staged, whole_sem, odd_sem, even_sem = rest[total + 8:]
+    staged = odd_staged, even_staged
     rows = whole.shape[1]
-    edge = Edge(plan, ODD, rows)
-    part = pl.ds(
-        pl.multiple_of(edge.first_block * BLOCK, BLOCK),
-        pl.multiple_of((edge.last_block - edge.first_block) * BLOCK, BLOCK))
-
-    def move(which, out):
-        inside, outside = whole.at[which, part], outs[which].at[part]
-        source, target = (inside, outside) if out else (outside, inside)
-        return pltpu.make_async_copy(source, target, whole_sem.at[which])
-
-    stage = functools.partial(
-        copy_pieces, levels, edge.level, staged, BLOCK, returned, staged_sem, False)
-
-    @pl.when(edge.sent > 0)
-    def _():
+    edges = [Edge(plan, kind, rows) for kind in (ODD, EVEN)]
+    stages = [
+        functools.partial(
+            copy_pieces, levels[kind], edges[kind].level, staged[kind], BLOCK, returned[kind],
+            sem, False)
+        for kind, sem in ((ODD, odd_sem), (EVEN, even_sem))
+    ]
+
+    ends = []
+    for edge, other in (edges, edges[::-1]):
+        meets = jnp.logical_not(edge.lower) & (other.sent > 0)
+        ends.append(jnp.where(
+            meets, jnp.minimum(edge.last_block, other.first_block), edge.last_block))
+
+    def move(kind, which, out, action):
+        first, last = edges[kind].first_block, ends[kind]
+
+        @pl.when((edges[kind].sent > 0) & (last > first))
+        def _():
+            part = pl.ds(
+                pl.multiple_of(first * BLOCK, BLOCK), pl.multiple_of((last - first) * BLOCK, BLOCK))
+            inside, outside = whole.at[which, part], outs[which].at[part]
+            source, target = (inside, outside) if out else (outside, inside)
+            action(pltpu.make_async_copy(source, target, whole_sem.at[kind, which]))
+
+    for stage in stages:
         stage(START)
-        for which in range(4):
-            move(which, False).start()
+    for which in range(4):
+        for kind in (ODD, EVEN):
+            move(kind, which, False, START)
+    for stage in stages:
         stage(WAIT)
-        for which in range(4):
-            columns = slice(which * HEAD_DIM, (which + 1) * HEAD_DIM)
-            move(which, False).wait()
+    for which in range(4):
+        columns = slice(which * HEAD_DIM, (which + 1) * HEAD_DIM)
+        for kind in (ODD, EVEN):
+            move(kind, which, False, WAIT)
+        for kind in (ODD, EVEN):
+            edge = edges[kind]
             overlay(whole, which, edge, edge.sent_head, edge.sent,
-                    returned_source(edge, staged, columns))
-            move(which, True).start()
-        for which in range(4):
-            move(which, True).wait()
-
-
-def merge_last(plan, returned, outs, levels):
+                    returned_source(edge, staged[kind], columns))
+        for kind in (ODD, EVEN):
+            move(kind, which, True, START)
+    for which in range(4):
+        for kind in (ODD, EVEN):
+            move(kind, which, True, WAIT)
+
+
+def merge_returned(plan, odd, even, outs, levels):
     rows, width = outs[0].shape
-    count = len(levels)
+    counts = [len(levels[ODD]), len(levels[EVEN])]
     return pl.pallas_call(
-        functools.partial(last_kernel, levels),
-        in_specs=[SCALARS] + [ANYWHERE] * (count + 4),
+        functools.partial(return_kernel, levels),
+        in_specs=[SCALARS] + [ANYWHERE] * (sum(counts) + 4),
         out_specs=[ANYWHERE] * 4,
-        out_shape=[jax.ShapeDtypeStruct((rows, width), jnp.bfloat16)] * 4,
-        input_output_aliases={1 + count + which: which for which in range(4)},
+        out_shape=[pltpu.HBM((rows, width), jnp.bfloat16)] * 4,
+        input_output_aliases={1 + sum(counts) + which: which for which in range(4)},
         scratch_shapes=[
             pltpu.VMEM((4, rows, width), jnp.bfloat16),
-            pltpu.VMEM((levels[-1] + 2 * BLOCK, 4 * HEAD_DIM), jnp.bfloat16),
-            pltpu.SemaphoreType.DMA((4,)),
-            pltpu.SemaphoreType.DMA((count,)),
+            pltpu.VMEM((levels[ODD][-1] + 2 * BLOCK, 4 * HEAD_DIM), jnp.bfloat16),
+            pltpu.VMEM((levels[EVEN][-1] + 2 * BLOCK, 4 * HEAD_DIM), jnp.bfloat16),
+            pltpu.SemaphoreType.DMA((2, 4)),
+            pltpu.SemaphoreType.DMA((counts[ODD],)),
+            pltpu.SemaphoreType.DMA((counts[EVEN],)),
         ],
         compiler_params=pltpu.CompilerParams(vmem_limit_bytes=VMEM_LIMIT),
-        name="merge_last",
-    )(plan, *returned, *outs)
+        name="merge_returned",
+    )(plan, *odd, *even, *in_hbm(outs))
 
 
 def swapped(value, kind):
@@ -598,44 +615,52 @@
     return lax.ppermute(value, "dp", pairs + [(after, before) for before, after in pairs])
 
 
-def swap_further(level, arrays, kind):
-    if not arrays:
-        return []
-
-    def send(used, arrays):
-        return [
-            swapped(array, kind) if number < used else jnp.zeros_like(array)
-            for number, array in enumerate(arrays)
-        ]
-
-    branches = [functools.partial(send, used) for used in range(len(arrays) + 1)]
-    return lax.switch(level[0], branches, list(arrays))
+def swap_further(choices, odd, even):
+    counts = [len(odd), len(even)]
+    if not sum(counts):
+        return [], []
+    pairs = [(first, second) for first in range(counts[0] + 1) for second in range(counts[1] + 1)]
+
+    def send(used, odd, even):
+        return tuple(
+            [
+                swapped(array, kind) if number == used[kind] else jnp.zeros_like(array)
+                for number, array in enumerate(arrays, start=1)
+            ]
+            for kind, arrays in ((ODD, odd), (EVEN, even))
+        )
+
+    index = 0
+    for choice, count in zip(choices, counts):
+        if count:
+            index = index * (count + 1) + choice[0]
+    branches = [functools.partial(send, pair) for pair in pairs]
+    return lax.switch(index, branches, list(odd), list(even))
 
 
 def body(queries, keys, values, out_grad, lengths):
     rows, width = queries.shape
     arrays = (queries, keys, values, out_grad)
     levels = [size_levels(kind, rows, width // HEAD_DIM) for kind in (ODD, EVEN)]
-    plan, (odd_level, even_level), (odd, even) = pack(
-        lengths, arrays, levels, lax.axis_size("dp"))
+    plan, choices, (odd, even) = pack(lengths, arrays, levels, lax.axis_size("dp"))
     even_first = swapped(even[0], EVEN)
     odd_first = swapped(odd[0], ODD)
     local = local_attention(lengths, arrays)
-    even_first, even_level, local = lax.optimization_barrier((even_first, even_level, local))
-    received = [even_first, *swap_further(even_level, even[1:], EVEN)]
-    back_even, kept_even = crossing_images(EVEN, plan, arrays, received, levels[EVEN])
-    odd_level, kept_even = lax.optimization_barrier((odd_level, kept_even))
-    received = [odd_first, *swap_further(odd_level, odd[1:], ODD)]
+    choices, local = lax.optimization_barrier((choices, local))
+    _, more = swap_further(choices, [], even[1:])
+    back_even, kept_even = crossing_images(EVEN, plan, arrays, [even_first, *more], levels[EVEN])
+    choices, kept_even = lax.optimization_barrier((choices, kept_even))
+    more, _ = swap_further(choices, odd[1:], [])
+    received = [odd_first, *more]
     first, received = lax.optimization_barrier((back_even[0], received))
-    back_first = swapped(first, EVEN)
+    even_first = swapped(first, EVEN)
     back_odd, kept_odd = crossing_images(ODD, plan, arrays, received, levels[ODD])
     odd_first = swapped(back_odd[0], ODD)
-    even_level, kept_odd = lax.optimization_barrier((even_level, kept_odd))
-    returned = [back_first, *swap_further(even_level, back_even[1:], EVEN)]
-    outs = merge_most(plan, kept_odd, kept_even, returned, local, levels[EVEN])
-    odd_level, outs = lax.optimization_barrier((odd_level, outs))
-    returned = [odd_first, *swap_further(odd_level, back_odd[1:], ODD)]
-    return tuple(merge_last(plan, returned, outs, levels[ODD]))
+    outs = merge_kept(plan, kept_odd, kept_even, local)
+    choices, outs = lax.optimization_barrier((choices, outs))
+    more_odd, more_even = swap_further(choices, back_odd[1:], back_even[1:])
+    return tuple(merge_returned(
+        plan, [odd_first, *more_odd], [even_first, *more_even], outs, levels))
 
 
 def solution(mesh):

time: 106 us -> 82.5 us (0.78)
  the two profiles are of different devices: /device:TPU:26 before, /device:TPU:11 now
where the time goes in v3:
time: 82.5 us; the launch traced here: 82.2 us
  Pallas kernels  43.3 us (52%)
  waiting for transfers between devices  20.3 us (25%)
  starting transfers between devices  10.6 us (13%)
  local copies, waits for them, and re-layouts  4.48 us (5%)
  between operations  3.4 us (4%)
    ppermute x6, waiting for transfers between devices, swapped(): lax.ppermute(value, 'dp', pairs + [(after, before) for before, after in p...  20.3 us
    pallas_call x2, Pallas kernels, crossing_images(): pl.pallas_call(functools.partial(crossing_kernel, levels, kind), in_specs...  17.9 us
    ppermute x6, starting transfers between devices, swapped(): lax.ppermute(value, 'dp', pairs + [(after, before) for before, after in p...  10.6 us
    pallas_call x1, Pallas kernels, local_attention(): pl.pallas_call(local_kernel, grid=(heads,), in_specs=[pl.BlockSpec(memory...  10.1 us
    pallas_call x1, Pallas kernels, merge_kept(): pl.pallas_call(keep_kernel, in_specs=[SCALARS] + [ANYWHERE] * 6, out_spec...  6.35 us
    pallas_call x1, Pallas kernels, merge_returned(): pl.pallas_call(functools.partial(return_kernel, levels), in_specs=[SCALAR...  4.48 us
    another operation x6, local copies, waits for them, and re-layouts  4.44 us
    pallas_call x1, Pallas kernels, pack(): pl.pallas_call(functools.partial(pack_kernel, levels, blocks), in_specs=[...  4.41 us
  transfers between devices with their start and end apart: 6, of which 3 were waited for; matrix products, arithmetic and copies ran while one was open for 5% of the time, Pallas kernels for 42%

profile of v3, /device:TPU:11, one launch (start us, length us, event | category | flops | bytes accessed | tf_op | source)
XLA Modules:
  0.0 82.2 jit_solution(3907079155680249229)
XLA Ops:
  0.6 0.0 copy-start.1
  0.6 4.4 %pack.1 = (s32[16]{0:T(128)}, s32[1]{0:T(128)}, s32[1]{0:T(128)}, bf16[576,512]{1,0:T(8,128)(2,1)}, bf16[192,512]{1,0:T(8,128)(2,1)}, /*index=5*/bf16[320,512]{1...) custom-call(s32[32]{0:T(128)} %lengths.3, bf16[512,768]{1,0:T(8,128)(2,1)} %query.5, ...), custom_call_target="tpu_custom_call" | custom-call | tf_op jit(solution)/shard_map/pack/pallas_call | solution.py:314
  5.1 3.0 %collective-permute-start.16 = (bf16[576,512]{1,0:T(8,128)(2,1)}, bf16[576,512]{1,0:T(8,128)(2,1)S(1)}, u32[]{:S(2)}, u32[]{:S(2)}) collective-permute-start(bf16[576,512]{1,0:T(8,128)(2,1)} %get-tuple-element.89), channel_id=1, source_target_pairs={{4,8},{12,16},{20,24},{8,4},{16,12},{24,20},{5,9},{13,17},{21,25},... | collective-permute-start | bytes 1769480 | tf_op jit(solution)/shard_map/ppermute | solution.py:615
  8.1 1.6 %collective-permute-start.17 = (bf16[576,512]{1,0:T(8,128)(2,1)}, bf16[576,512]{1,0:T(8,128)(2,1)S(1)}, u32[]{:S(2)}, u32[]{:S(2)}) collective-permute-start(bf16[576,512]{1,0:T(8,128)(2,1)} %get-tuple-element.102), channel_id=1, source_target_pairs={{0,4},{8,12},{16,20},{24,28},{4,0},{12,8},{20,16},{28,24},{1,5},{9... | collective-permute-start | bytes 1769480 | tf_op jit(solution)/shard_map/ppermute | solution.py:615
  9.6 0.0 copy-done.1
  9.6 10.1 %local_images.1 = (bf16[512,768]{1,0:T(8,128)(2,1)}, bf16[512,768]{1,0:T(8,128)(2,1)}, bf16[512,768]{1,0:T(8,128)(2,1)}, bf16[512,768]{1,0:T(8,128)(2,1)}) custom-call(s32[32]{0:T(128)S(1)} %copy-done.1, bf16[512,768]{1,0:T(8,128)(2,1)} %query.5, bf16[512,768]{1,0:T(8,128)(2,1)} %key.5, bf16[512,768]{1,0:T(8,128)(2,1)} %value.5, bf16[512,768]{1,0:T(8,128)(2,1)} %grad.5), custom_call_target="tpu_custom_call" | custom-call | flops 2415919104 | bytes 6291456 | tf_op jit(solution)/shard_map/local_images/pallas_call | solution.py:221
  20.4 0.0 copy-done.5
  20.4 0.0 copy-done.9
  20.4 8.9 %conditional.3 = (bf16[192,512]{1,0:T(8,128)(2,1)}, bf16[320,512]{1,0:T(8,128)(2,1)}) conditional(s32[]{:T(128)} %bitcast, () %tuple.72, bf16[192,512]{1,0:T(8,128)(2,1)S(1)} %copy-done.9, bf16[320,512]{1,0:T(8,128)(2,1)S(1)} %copy-done.5), branch_computations={%region_0.0_spmd, %region_1.0_spmd, %region_2.0_spmd} | conditional | bytes 1507386 | solution.py:638
  20.4 1.9 %collective-permute-start = (bf16[192,512]{1,0:T(8,128)(2,1)S(1)}, bf16[192,512]{1,0:T(8,128)(2,1)}, u32[]{:S(2)}, u32[]{:S(2)}) collective-permute-start(bf16[192,512]{1,0:T(8,128)(2,1)S(1)} %param.1), channel_id=1, source_target_pairs={{4,8},{12,16},{20,24},{8,4},{16,12},{24,20},{5,9},{13,17},{21,25},... | collective-permute-start | bytes 589832 | tf_op jit(solution)/shard_map/cond/branch_1_fun/ppermute | solution.py:615
  22.3 6.2 %collective-permute-done = bf16[192,512]{1,0:T(8,128)(2,1)} collective-permute-done((bf16[192,512]{1,0:T(8,128)(2,1)S(1)}, bf16[192,512]{1,0:T(8,128)(2,1)}, u32[]{:S(2)}, u32[]{:S(2)}) %collective-permute-start) | collective-permute-done | bytes 196640 | tf_op jit(solution)/shard_map/cond/branch_1_fun/ppermute | solution.py:615
  28.5 0.8 broadcast.50
  29.3 0.0 collective-permute-done.16.rest_0_
  29.3 0.0 copy-done
  29.3 11.1 %even_edge_images.1 = (bf16[576,512]{1,0:T(8,128)(2,1)}, bf16[192,512]{1,0:T(8,128)(2,1)}, bf16[320,512]{1,0:T(8,128)(2,1)}, bf16[6,512,512]{2,1,0:T(8,128)(2,1)}) custom-call(s32[16]{0:T(128)S(1)} %copy-done, bf16[512,768]{1,0:T(8,128)(2,1)} %query.5, bf16[512,768]{1,0:T(8,128)(2,1)} %key.5, bf16[512,768]{1,0:T(8,128)(2,1)} %value.5, ...), custom_call_target="tpu_custom_call" | custom-call | flops 2415919104 | bytes 6291456 | tf_op jit(solution)/shard_map/even_edge_images/pallas_call | solution.py:417
  41.1 1.5 %conditional.4 = (bf16[192,512]{1,0:T(8,128)(2,1)}, bf16[320,512]{1,0:T(8,128)(2,1)}) conditional(s32[]{:T(128)} %bitcast.1, () %tuple.74, bf16[192,512]{1,0:T(8,128)(2,1)S(1)} %copy-done.8, bf16[320,512]{1,0:T(8,128)(2,1)S(1)} %copy-done.4), branch_computations={%region_3.0_spmd, %region_4.0_spmd, %region_5.0_spmd} | conditional | bytes 1507386 | solution.py:638
  41.1 0.7 broadcast.52
  41.8 0.8 broadcast.53
  42.6 0.0 collective-permute-done.17.rest_0_
  42.6 1.9 %collective-permute-start.19 = (bf16[576,512]{1,0:T(8,128)(2,1)}, bf16[576,512]{1,0:T(8,128)(2,1)S(1)}, u32[]{:S(2)}, u32[]{:S(2)}) collective-permute-start(bf16[576,512]{1,0:T(8,128)(2,1)} %get-tuple-element.133), channel_id=1, source_target_pairs={{4,8},{12,16},{20,24},{8,4},{16,12},{24,20},{5,9},{13,17},{21,25},... | collective-permute-start | bytes 1769480 | tf_op jit(solution)/shard_map/ppermute | solution.py:615
  44.5 6.9 %odd_edge_images.1 = (bf16[576,512]{1,0:T(8,128)(2,1)}, bf16[192,512]{1,0:T(8,128)(2,1)}, bf16[320,512]{1,0:T(8,128)(2,1)}, bf16[6,512,512]{2,1,0:T(8,128)(2,1)}) custom-call(s32[16]{0:T(128)S(1)} %copy-done, bf16[512,768]{1,0:T(8,128)(2,1)} %query.5, bf16[512,768]{1,0:T(8,128)(2,1)} %key.5, bf16[512,768]{1,0:T(8,128)(2,1)} %value.5, bf16[512,768]{1,0:T(8,128)(2,1)} %grad.5, ...), custom_call_target="tpu_custom_call" | custom-call | flops 2415919104 | bytes 6291456 | tf_op jit(solution)/shard_map/odd_edge_images/pallas_call | solution.py:417
  51.4 0.3 collective-permute-start.18
  51.7 6.4 %merge_kept.1 = (bf16[512,768]{1,0:T(8,128)(2,1)}, bf16[512,768]{1,0:T(8,128)(2,1)}, bf16[512,768]{1,0:T(8,128)(2,1)}, bf16[512,768]{1,0:T(8,128)(2,1)}) custom-call(s32[16]{0:T(128)S(1)} %copy-done, bf16[6,512,512]{2,1,0:T(8,128)(2,1)} %get-tuple-element.115.kept_odd, bf16[6,512,512]{2,1,0:T(8,128)(2,1)} %get-tuple-element.116.kept_even, ...), custom_call_target="tpu_custom_call" | custom-call | bytes 12582912 | tf_op jit(solution)/shard_map/merge_kept/pallas_call | solution.py:515
  59.4 9.8 %conditional.5 = (bf16[192,512]{1,0:T(8,128)(2,1)}, bf16[320,512]{1,0:T(8,128)(2,1)}, bf16[192,512]{1,0:T(8,128)(2,1)}, bf16[320,512]{1,0:T(8,128)(2,1)}) conditional(s32[]{:T(128)} %bitcast.2, () %tuple.77, bf16[192,512]{1,0:T(8,128)(2,1)S(1)} %copy-done.6, bf16[320,512]{1,0:T(8,128)(2,1)S(1)} %copy-done.2, ...), branch_computations={%region_6.0_spmd, %region_7.0_spmd, %region_8.0_spmd, %region_9.0_... | conditional | bytes 3014772 | solution.py:638
  59.5 1.9 %collective-permute-start.4 = (bf16[192,512]{1,0:T(8,128)(2,1)S(1)}, bf16[192,512]{1,0:T(8,128)(2,1)}, u32[]{:S(2)}, u32[]{:S(2)}) collective-permute-start(bf16[192,512]{1,0:T(8,128)(2,1)S(1)} %param.7), channel_id=1, source_target_pairs={{4,8},{12,16},{20,24},{8,4},{16,12},{24,20},{5,9},{13,17},{21,25},... | collective-permute-start | bytes 589832 | tf_op jit(solution)/shard_map/cond/branch_1_fun/ppermute | solution.py:615
  61.4 5.6 %collective-permute-done.4 = bf16[192,512]{1,0:T(8,128)(2,1)} collective-permute-done((bf16[192,512]{1,0:T(8,128)(2,1)S(1)}, bf16[192,512]{1,0:T(8,128)(2,1)}, u32[]{:S(2)}, u32[]{:S(2)}) %collective-permute-start.4) | collective-permute-done | bytes 196640 | tf_op jit(solution)/shard_map/cond/branch_1_fun/ppermute | solution.py:615
  67.0 0.7 broadcast.58
  67.7 0.8 broadcast.59.clone
  68.5 0.8 broadcast.59
  69.2 0.0 collective-permute-done.19.rest_3_
  69.2 8.5 %collective-permute-done.18.rest_0_ = bf16[576,512]{1,0:T(8,128)(2,1)S(1)} collective-permute-done((bf16[576,512]{1,0:T(8,128)(2,1)}, bf16[576,512]{1,0:T(8,128)(2,1)S(1)}, u32[]{:S(2)}, u32[]{:S(2)}) %collective-permute-start.18) | collective-permute-done | bytes 589856 | tf_op jit(solution)/shard_map/ppermute | solution.py:615
  77.7 4.5 %merge_returned.1 = (bf16[512,768]{1,0:T(8,128)(2,1)}, bf16[512,768]{1,0:T(8,128)(2,1)}, bf16[512,768]{1,0:T(8,128)(2,1)}, bf16[512,768]{1,0:T(8,128)(2,1)}) custom-call(s32[16]{0:T(128)S(1)} %copy-done, bf16[576,512]{1,0:T(8,128)(2,1)S(1)} %collective-permute-done.18.rest_0_, ...), custom_call_target="tpu_custom_call", output_to_operand_aliasing={{0}: (7, {}), {1}: (8, {}), {2}: (9, {}), {3}: (10, {})} | custom-call | tf_op jit(solution)/shard_map/merge_returned/pallas_call | solution.py:593
  (15 shorter events, 0.0 us)
Async XLA Ops:
  0.6 9.0 %copy-start.1 = (s32[32]{0:T(128)S(1)}, s32[32]{0:T(128)}, u32[]{:S(2)}) copy-start(s32[32]{0:T(128)} %lengths.3) | copy-start | bytes 388
  5.1 24.3 %collective-permute-start.16 = (bf16[576,512]{1,0:T(8,128)(2,1)}, bf16[576,512]{1,0:T(8,128)(2,1)S(1)}, u32[]{:S(2)}, u32[]{:S(2)}) collective-permute-start(bf16[576,512]{1,0:T(8,128)(2,1)} %get-tuple-element.89), channel_id=1, source_target_pairs={{4,8},{12,16},{20,24},{8,4},{16,12},{24,20},{5,9},{13,17},{21,25},... | collective-permute-start | bytes 1769480 | tf_op jit(solution)/shard_map/ppermute | solution.py:615
  8.1 34.5 %collective-permute-start.17 = (bf16[576,512]{1,0:T(8,128)(2,1)}, bf16[576,512]{1,0:T(8,128)(2,1)S(1)}, u32[]{:S(2)}, u32[]{:S(2)}) collective-permute-start(bf16[576,512]{1,0:T(8,128)(2,1)} %get-tuple-element.102), channel_id=1, source_target_pairs={{0,4},{8,12},{16,20},{24,28},{4,0},{12,8},{20,16},{28,24},{1,5},{9... | collective-permute-start | bytes 1769480 | tf_op jit(solution)/shard_map/ppermute | solution.py:615
  9.6 10.7 %copy-start.5 = (bf16[320,512]{1,0:T(8,128)(2,1)S(1)}, bf16[320,512]{1,0:T(8,128)(2,1)}, u32[]{:S(2)}) copy-start(bf16[320,512]{1,0:T(8,128)(2,1)} %get-tuple-element.98) | copy-start | bytes 983044
  9.6 10.8 %copy-start.9 = (bf16[192,512]{1,0:T(8,128)(2,1)S(1)}, bf16[192,512]{1,0:T(8,128)(2,1)}, u32[]{:S(2)}) copy-start(bf16[192,512]{1,0:T(8,128)(2,1)} %get-tuple-element.97) | copy-start | bytes 589828
  9.6 19.7 %copy-start = (s32[16]{0:T(128)S(1)}, s32[16]{0:T(128)}, u32[]{:S(2)}) copy-start(s32[16]{0:T(128)} %get-tuple-element.88.plan) | copy-start | bytes 196
  20.4 8.1 %collective-permute-start = (bf16[192,512]{1,0:T(8,128)(2,1)S(1)}, bf16[192,512]{1,0:T(8,128)(2,1)}, u32[]{:S(2)}, u32[]{:S(2)}) collective-permute-start(bf16[192,512]{1,0:T(8,128)(2,1)S(1)} %param.1), channel_id=1, source_target_pairs={{4,8},{12,16},{20,24},{8,4},{16,12},{24,20},{5,9},{13,17},{21,25},... | collective-permute-start | bytes 589832 | tf_op jit(solution)/shard_map/cond/branch_1_fun/ppermute | solution.py:615
  29.3 11.8 %copy-start.4 = (bf16[320,512]{1,0:T(8,128)(2,1)S(1)}, bf16[320,512]{1,0:T(8,128)(2,1)}, u32[]{:S(2)}) copy-start(bf16[320,512]{1,0:T(8,128)(2,1)} %get-tuple-element.107) | copy-start | bytes 983044
  29.3 11.8 %copy-start.8 = (bf16[192,512]{1,0:T(8,128)(2,1)S(1)}, bf16[192,512]{1,0:T(8,128)(2,1)}, u32[]{:S(2)}) copy-start(bf16[192,512]{1,0:T(8,128)(2,1)} %get-tuple-element.106) | copy-start | bytes 589828
  42.6 26.6 %collective-permute-start.19 = (bf16[576,512]{1,0:T(8,128)(2,1)}, bf16[576,512]{1,0:T(8,128)(2,1)S(1)}, u32[]{:S(2)}, u32[]{:S(2)}) collective-permute-start(bf16[576,512]{1,0:T(8,128)(2,1)} %get-tuple-element.133), channel_id=1, source_target_pairs={{4,8},{12,16},{20,24},{8,4},{16,12},{24,20},{5,9},{13,17},{21,25},... | collective-permute-start | bytes 1769480 | tf_op jit(solution)/shard_map/ppermute | solution.py:615
  51.4 26.3 %collective-permute-start.18 = (bf16[576,512]{1,0:T(8,128)(2,1)}, bf16[576,512]{1,0:T(8,128)(2,1)S(1)}, u32[]{:S(2)}, u32[]{:S(2)}) collective-permute-start(bf16[576,512]{1,0:T(8,128)(2,1)} %get-tuple-element.113), channel_id=1, source_target_pairs={{0,4},{8,12},{16,20},{24,28},{4,0},{12,8},{20,16},{28,24},{1,5},{9... | collective-permute-start | bytes 1769480 | tf_op jit(solution)/shard_map/ppermute | solution.py:615
  51.7 7.7 %copy-start.2 = (bf16[320,512]{1,0:T(8,128)(2,1)S(1)}, bf16[320,512]{1,0:T(8,128)(2,1)}, u32[]{:S(2)}) copy-start(bf16[320,512]{1,0:T(8,128)(2,1)} %get-tuple-element.128) | copy-start | bytes 983044
  51.7 7.7 %copy-start.3 = (bf16[320,512]{1,0:T(8,128)(2,1)S(1)}, bf16[320,512]{1,0:T(8,128)(2,1)}, u32[]{:S(2)}) copy-start(bf16[320,512]{1,0:T(8,128)(2,1)} %get-tuple-element.130) | copy-start | bytes 983044
  51.7 7.7 %copy-start.6 = (bf16[192,512]{1,0:T(8,128)(2,1)S(1)}, bf16[192,512]{1,0:T(8,128)(2,1)}, u32[]{:S(2)}) copy-start(bf16[192,512]{1,0:T(8,128)(2,1)} %get-tuple-element.127) | copy-start | bytes 589828
  51.7 7.7 %copy-start.7 = (bf16[192,512]{1,0:T(8,128)(2,1)S(1)}, bf16[192,512]{1,0:T(8,128)(2,1)}, u32[]{:S(2)}) copy-start(bf16[192,512]{1,0:T(8,128)(2,1)} %get-tuple-element.129) | copy-start | bytes 589828
  59.5 7.5 %collective-permute-start.4 = (bf16[192,512]{1,0:T(8,128)(2,1)S(1)}, bf16[192,512]{1,0:T(8,128)(2,1)}, u32[]{:S(2)}, u32[]{:S(2)}) collective-permute-start(bf16[192,512]{1,0:T(8,128)(2,1)S(1)} %param.7), channel_id=1, source_target_pairs={{4,8},{12,16},{20,24},{8,4},{16,12},{24,20},{5,9},{13,17},{21,25},... | collective-permute-start | bytes 589832 | tf_op jit(solution)/shard_map/cond/branch_1_fun/ppermute | solution.py:615
